TPU v7x, 32 devices: a whole 2x2x4 slice. The times are simulated.
32 devices in a mesh: pipe: 4 (over y, core), dp: 8 (over z, x).
Axes of the slice: x: 2, y: 2, z: 4, core: 2. Of those that a mesh axis runs over, the one named last changes fastest.
Arguments:
- block_input: bfloat16 [8, 1024, 768], P('dp', 'pipe'), may hold values from -6 to 6
- ln_gain: float32 [4, 2, 768], P('pipe'), may hold values from 0.5 to 1.5
- ln_bias: float32 [4, 2, 768], P('pipe'), may hold values from -0.6 to 0.6
- tm_mix: float32 [4, 3, 768], P('pipe'), may hold values from 0 to 1
- cm_mix: float32 [4, 2, 768], P('pipe'), may hold values from 0 to 1
- time_decay: float32 [4, 768], P('pipe'), may hold values from -5 to 1
- time_first: float32 [4, 768], P('pipe'), may hold values from -1 to 1
- tm_in: bfloat16 [4, 3, 768, 768], P('pipe'), may hold values from -0.21875 to 0.21875
- tm_out: bfloat16 [4, 768, 768], P('pipe'), may hold values from -0.4375 to 0.4375
- cm_key: bfloat16 [4, 768, 3072], P('pipe'), may hold values from -0.21875 to 0.21875
- cm_value: bfloat16 [4, 3072, 768], P('pipe'), may hold values from -0.109375 to 0.109375
- cm_recept: bfloat16 [4, 768, 768], P('pipe'), may hold values from -0.21875 to 0.21875
- wkv_num: float32 [4, 8, 768], P('pipe', 'dp'), may hold values from -6 to 6
- wkv_den: float32 [4, 8, 768], P('pipe', 'dp'), may hold values from 0.5 to 4
- last_rows: float32 [4, 2, 8, 768], P('pipe', None, 'dp'), may hold values from -6 to 6
- cotangent: bfloat16 [8, 1024, 768], P('dp', 'pipe'), may hold values from -6 to 6
Outputs:
- block_output: float32 [8, 1024, 768], P('dp', 'pipe')
- grad_block_input: float32 [8, 1024, 768], P('dp', 'pipe')
- grad_ln_gain: float32 [4, 2, 768], P('pipe')
- grad_ln_bias: float32 [4, 2, 768], P('pipe')
- grad_tm_mix: float32 [4, 3, 768], P('pipe')
- grad_cm_mix: float32 [4, 2, 768], P('pipe')
- grad_time_decay: float32 [4, 768], P('pipe')
- grad_time_first: float32 [4, 768], P('pipe')
- grad_tm_in: float32 [4, 3, 768, 768], P('pipe')
- grad_tm_out: float32 [4, 768, 768], P('pipe')
- grad_cm_key: float32 [4, 768, 3072], P('pipe')
- grad_cm_value: float32 [4, 3072, 768], P('pipe')
- grad_cm_recept: float32 [4, 768, 768], P('pipe')
- final_num: float32 [4, 8, 768], P('pipe', 'dp')
- final_den: float32 [4, 8, 768], P('pipe', 'dp')
- final_rows: float32 [4, 2, 8, 768], P('pipe', None, 'dp')
All inputs are finite; a program needn't handle non-finite values.
Results may differ from a plain program's by a relative error of at most 0.02.
Values may be sent and summed in bfloat16 or wider, within the bound.
A program may use at most 512 MiB of HBM per device.

v0:
```python
import functools

import jax
import jax.numpy as jnp
from jax import lax
from jax.experimental import pallas as pl
from jax.experimental.pallas import tpu as pltpu
from jax.sharding import PartitionSpec as P

MESH = pl.DeviceIdType.MESH
BF, F32 = jnp.bfloat16, jnp.float32
TOKENS = 128
SPLIT = 3
LAG = 2
VMEM_BYTES = 62 * 1024 * 1024


def position():
    p, i = lax.axis_index("pipe"), lax.axis_index("dp")
    y = lax.div(p, 2)
    k = p - 2 * y
    first = 2 * lax.div(i, 2)
    s = i - first
    return p, i, y, k, first, s, lax.rem(s + y, 2)


def home(layer, k, first):
    y = lax.div(layer, 2)
    return 2 * y + k, first + lax.rem(layer - y, 2)


def local(src, dst, sem):
    return pltpu.make_async_copy(src, dst, sem)


def remote(src, dst, send, recv, p, i):
    return pltpu.make_async_remote_copy(
        src_ref=src, dst_ref=dst, send_sem=send, recv_sem=recv, device_id=(p, i), device_id_type=MESH
    )


def drain(ref, sem):
    pltpu.make_async_copy(ref, ref, sem).wait()


def dot(a, b):
    return lax.dot_general(a, b, (((1,), (0,)), ((), ())), preferred_element_type=F32)


def dot_t(a, b):
    return lax.dot_general(a, b, (((1,), (1,)), ((), ())), preferred_element_type=F32)


def later(v, row):
    at = lax.broadcasted_iota(jnp.int32, v.shape, 0)
    return jnp.where(at == 0, row, pltpu.roll(v, 1, 0))


def earlier(v, row):
    n = v.shape[0]
    at = lax.broadcasted_iota(jnp.int32, v.shape, 0)
    return jnp.where(at == n - 1, row, pltpu.roll(v, n - 1, 0))


def scan_down(v, rate):
    n, by = v.shape[0], 1
    while by < n:
        fade = jnp.exp(-float(by) * rate)
        if by < 8:
            at = lax.broadcasted_iota(jnp.int32, v.shape, 0)
            v = v + jnp.where(at >= by, fade * pltpu.roll(v, by, 0), 0.0)
        else:
            v = jnp.concatenate([v[:by], v[by:] + fade * v[: n - by]], axis=0)
        by *= 2
    return v


def scan_up(v, rate):
    n, by = v.shape[0], 1
    while by < n:
        fade = jnp.exp(-float(by) * rate)
        if by < 8:
            at = lax.broadcasted_iota(jnp.int32, v.shape, 0)
            v = v + jnp.where(at < n - by, fade * pltpu.roll(v, n - by, 0), 0.0)
        else:
            v = jnp.concatenate([v[: n - by] + fade * v[by:], v[n - by :]], axis=0)
        by *= 2
    return v


def centred(v):
    c = v - jnp.mean(v, axis=-1, keepdims=True)
    r = lax.rsqrt(jnp.mean(c * c, axis=-1, keepdims=True) + 1e-05)
    return c * r, r


def layers_kernel(
    npipe,
    x_hbm, cot_hbm, gain_hbm, bias_hbm, tmix_hbm, cmix_hbm, decay_hbm, first_hbm, num_hbm, den_hbm, rows_hbm,
    win_hbm, wout_hbm, wck_hbm, wcv_hbm, wcr_hbm,
    xo, go, small, fin_num, fin_den, fin_rows, ob, gb, turned,
    w, gain, bias, tmix, cmix, decay, bonus_s, num_s, den_s, rows_s, inbox, gbox,
    e_s, v_s, n_s, d_s, s_s, xh1, xh2, s2_s, c2_s, relu, r1, r2, car1, car2, back, acc, xst, gst,
    w_send, w_recv, in_send, in_recv, g_send, g_recv, x0_send, cot_send, ob_recv, gb_recv,
    st_send, st_recv, fin_send, fin_recv, x_sem, go_sem, relu_sem, turn_out, turn_in,
):
    p, i, y, k, first, s, m_chip = position()
    layer = 2 * y + m_chip
    last = npipe - 1
    nm, nt, width = inbox.shape
    nq = relu.shape[1] // nt
    per = x_hbm.shape[1] // nt
    nblocks = w.shape[0]
    key, val, rec = 4, 4 + nq, 4 + 2 * nq

    weights = [(gain_hbm.at[0], gain), (bias_hbm.at[0], bias), (tmix_hbm.at[0], tmix), (cmix_hbm.at[0], cmix),
               (decay_hbm, decay), (first_hbm, bonus_s)]
    base = len(weights)
    order = [0, 1, 2, 3] + [at for q in range(nq) for at in (key + q, val + q)] + [rec]
    source = {rec: wcr_hbm.at[0], 3: wout_hbm.at[0]}
    for c in range(3):
        source[c] = win_hbm.at[0, c]
    for q in range(nq):
        source[key + q] = wck_hbm.at[0, :, q * width : (q + 1) * width]
        source[val + q] = wcv_hbm.at[0, q * width : (q + 1) * width]
    weights += [(source[at], w.at[at]) for at in order]
    place = {at: base + n for n, at in enumerate(order)}
    owner = k == m_chip

    @pl.when(owner)
    def _():
        for a, (src, dst) in enumerate(weights):
            local(src, dst, w_recv.at[a]).start()

    barrier = pltpu.get_barrier_semaphore()
    for step in range(1, 2 * npipe):
        at = lax.rem(2 * p + s + step, 2 * npipe)
        op = lax.div(at, 2)
        pl.semaphore_signal(barrier, inc=1, device_id=(op, first + at - 2 * op), device_id_type=MESH)
    pl.semaphore_wait(barrier, 2 * npipe - 1)

    ip, ii = home(0, s, first)
    in_self = jnp.logical_and(ip == p, ii == i)
    cp, ci = home(last, s, first)
    cot_self = jnp.logical_and(cp == p, ci == i)
    tp, ti = home(p, s, first)
    st_self = jnp.logical_and(tp == p, ti == i)

    def give(src, dst, send, recv, dp, di, mine):
        @pl.when(mine)
        def _():
            local(src, dst, recv).start()

        @pl.when(jnp.logical_not(mine))
        def _():
            remote(src, dst, send, recv, dp, di).start()

    states = ((num_hbm.at[0], num_s), (den_hbm.at[0], den_s), (rows_hbm.at[0, :, 0], rows_s))

    @pl.when(owner)
    def _():
        for a, (src, dst) in enumerate(weights[:base]):
            remote(src, dst, w_send.at[a], w_recv.at[a], 2 * y + 1 - k, i).start()

    for u in range(per):
        give(x_hbm.at[0, pl.ds(u * nt, nt)], inbox.at[p * per + u], x0_send.at[u], in_recv.at[p * per + u], ip, ii, in_self)
    for a, (src, dst) in enumerate(states):
        give(src, dst, st_send.at[a], st_recv.at[a], tp, ti, st_self)

    @pl.when(owner)
    def _():
        for a, (src, dst) in enumerate(weights[base:]):
            remote(src, dst, w_send.at[base + a], w_recv.at[base + a], 2 * y + 1 - k, i).start()

    for u in range(per):
        give(cot_hbm.at[0, pl.ds(u * nt, nt)], gbox.at[p * per + u], cot_send.at[u], g_recv.at[p * per + u], cp, ci, cot_self)

    for a in range(base):
        drain(weights[a][1], w_recv.at[a])
    for a, (src, dst) in enumerate(states):
        drain(dst, st_recv.at[a])
    np_, ni = home(layer + 1, k, first)
    bp, bi = home(layer - 1, k, first)
    rate = jnp.exp(decay[...])
    bonus = jnp.exp(bonus_s[...])
    fade = jnp.exp(-rate)

    @pl.when(layer == last)
    def _():
        for at in order:
            drain(w.at[at], w_recv.at[place[at]])

        def turn(at, none):
            slot = lax.rem(at, 2)

            @pl.when(at >= 2)
            def _():
                drain(gst.at[slot, pl.ds(0, width)], turn_out.at[slot])

            gst[slot, 0:width] = w[at].T
            local(gst.at[slot, pl.ds(0, width)], turned.at[at], turn_out.at[slot]).start()
            return none

        lax.fori_loop(0, nblocks, turn, 0)
        for slot in range(2):
            drain(gst.at[slot, pl.ds(0, width)], turn_out.at[slot])

    def forward(m, none, begin=False):
        slot = lax.rem(m, 2)

        def ready(*blocks):
            if begin:

                @pl.when(layer < last)
                def _():
                    for at in blocks:
                        drain(w.at[at], w_recv.at[place[at]])

        if not begin:

            @pl.when(m >= 2)
            def _():
                drain(xst.at[slot], x_sem.at[slot])

        drain(inbox.at[m], in_recv.at[m])
        h = inbox[m].astype(F32)
        xh, rs = centred(h)
        xh1[m] = xh.astype(BF)
        r1[m] = rs
        xn = xh * gain[0:1] + bias[0:1]
        prev = rows_s[0:1]
        car1[m, 0:1] = prev
        xp = later(xn, prev)
        rows_s[0:1] = xn[nt - 1 :]
        d = xn - xp
        proj = []
        for c in range(3):
            mixed = (xp + tmix[c : c + 1] * d).astype(BF)
            xst[slot, c * nt : (c + 1) * nt] = mixed
            ready(c)
            proj.append(dot(mixed, w[c]))
        e = jnp.exp(proj[0])
        v = proj[1]
        ev = e * v
        num = scan_down(later(ev, num_s[...]), rate)
        den = scan_down(later(e, den_s[...]), rate)
        num_s[...] = fade * num[nt - 1 :] + ev[nt - 1 :]
        den_s[...] = fade * den[nt - 1 :] + e[nt - 1 :]
        e_s[m] = e
        v_s[m] = v
        n_s[m] = num
        d_s[m] = den
        b = bonus * e
        gate = jax.nn.sigmoid(proj[2])
        s_s[m] = gate.astype(BF)
        gated = (gate * ((num + b * v) / (den + b))).astype(BF)
        xst[slot, 3 * nt : 4 * nt] = gated
        ready(3)
        mid = h + dot(gated, w[3])
        xh, rs = centred(mid)
        xh2[m] = xh.astype(BF)
        r2[m] = rs
        xn = xh * gain[1:2] + bias[1:2]
        prev = rows_s[1:2]
        car2[m, 0:1] = prev
        xp = later(xn, prev)
        rows_s[1:2] = xn[nt - 1 :]
        d = xn - xp
        mixed0 = (xp + cmix[0:1] * d).astype(BF)
        mixed1 = (xp + cmix[1:2] * d).astype(BF)
        xst[slot, 4 * nt : 5 * nt] = mixed0
        xst[slot, 5 * nt : 6 * nt] = mixed1
        out = None
        for q in range(nq):
            ready(key + q)
            r = jnp.maximum(dot(mixed0, w[key + q]), 0.0)
            relu[m, q * nt : (q + 1) * nt] = r.astype(BF)
            ready(val + q)
            part = dot((r * r).astype(BF), w[val + q])
            out = part if out is None else out + part
        ready(rec)
        gate = jax.nn.sigmoid(dot(mixed1, w[rec]))
        s2_s[m] = gate.astype(BF)
        c2_s[m] = (out * gate * (1.0 - gate)).astype(BF)
        inbox[m] = (mid + gate * out).astype(BF)

        @pl.when(layer < last)
        def _():
            remote(inbox.at[m], inbox.at[m], in_send.at[m], in_recv.at[m], np_, ni).start()

        @pl.when(layer == last)
        def _():
            q = lax.div(m, per)
            u = m - q * per
            mine = jnp.logical_and(q == p, first + k == i)
            give(inbox.at[m], ob.at[pl.ds(pl.multiple_of(u * nt, nt), nt)], in_send.at[m], ob_recv.at[u], q, first + k, mine)

        local(xst.at[slot], xo.at[m, pl.ds(0, 6 * nt)], x_sem.at[slot]).start()
        local(relu.at[m], xo.at[m, pl.ds(6 * nt, nq * nt)], relu_sem.at[m]).start()
        return none

    forward(0, 0, True)
    lax.fori_loop(1, nm, forward, 0)

    wanted = [at for q in range(nq) for at in (val + q, key + q)] + [rec, 3, 0, 1, 2]

    @pl.when(layer == last)
    def _():
        for at in wanted:
            local(turned.at[at], w.at[at], turn_in.at[at]).start()

    finals = ((num_s, fin_num.at[0]), (den_s, fin_den.at[0]), (rows_s, fin_rows.at[0, :, 0]))
    fp, fi = layer, first + k
    fin_self = jnp.logical_and(fp == p, fi == i)
    for a, (src, dst) in enumerate(finals):
        give(src, dst, fin_send.at[a], fin_recv.at[a], fp, fi, fin_self)

    @pl.when(layer < last)
    def _():
        def turn(at, none):
            w[at] = w[at].T
            return none

        lax.fori_loop(0, nblocks, turn, 0)

    back[...] = jnp.zeros_like(back)
    acc[...] = jnp.zeros_like(acc)

    def mix_back(grads, xh, rs, prev, gain_row, bias_row, mixes, back_at, acc_gain, acc_bias, acc_mix):
        xn = xh * gain_row + bias_row
        d = xn - later(xn, prev)
        here, total = None, None
        for at, (g, mix) in enumerate(zip(grads, mixes)):
            acc[acc_mix + at : acc_mix + at + 1] += jnp.sum(g * d, axis=0, keepdims=True)
            here = g * mix if here is None else here + g * mix
            total = g if total is None else total + g
        shifted = total - here
        gx = here + earlier(shifted, back[back_at : back_at + 1])
        back[back_at : back_at + 1] = shifted[0:1]
        acc[acc_gain : acc_gain + 1] += jnp.sum(gx * xh, axis=0, keepdims=True)
        acc[acc_bias : acc_bias + 1] += jnp.sum(gx, axis=0, keepdims=True)
        gp = gx * gain_row
        return rs * (gp - jnp.mean(gp, axis=-1, keepdims=True) - xh * jnp.mean(gp * xh, axis=-1, keepdims=True))

    def backward(step, none, begin=False):
        m = nm - 1 - step
        slot = lax.rem(step, 2)

        def ready(*blocks):
            if begin:

                @pl.when(layer == last)
                def _():
                    for at in blocks:
                        drain(w.at[at], turn_in.at[at])

        if not begin:

            @pl.when(step >= 2)
            def _():
                drain(gst.at[slot], go_sem.at[slot])

        drain(gbox.at[m], g_recv.at[m])
        g = gbox[m].astype(F32)
        gvo = (g * s2_s[m].astype(F32)).astype(BF)
        grp = (g * c2_s[m].astype(F32)).astype(BF)
        gst[slot, (4 + nq) * nt : (5 + nq) * nt] = gvo
        gst[slot, (5 + nq) * nt : (6 + nq) * nt] = grp
        gm0 = None
        for q in range(nq):
            ready(val + q)
            gs = dot(gvo, w[val + q])
            gk = (gs * (2.0 * relu[m, q * nt : (q + 1) * nt].astype(F32))).astype(BF)
            gst[slot, (4 + q) * nt : (5 + q) * nt] = gk
            ready(key + q)
            part = dot(gk, w[key + q])
            gm0 = part if gm0 is None else gm0 + part
        ready(rec)
        gm1 = dot(grp, w[rec])
        gmid = g + mix_back(
            (gm0, gm1), xh2[m].astype(F32), r2[m], car2[m, 0:1], gain[1:2], bias[1:2], (cmix[0:1], cmix[1:2]), 3, 1, 3, 7
        )
        gbranch = gmid.astype(BF)
        gst[slot, 3 * nt : 4 * nt] = gbranch
        ready(3)
        gg = dot(gbranch, w[3])
        gate = s_s[m].astype(F32)
        e, v, num, den = e_s[m], v_s[m], n_s[m], d_s[m]
        b = bonus * e
        inv = 1.0 / (den + b)
        wkv = (num + b * v) * inv
        gn = gg * gate * inv
        gr = gg * wkv * gate * (1.0 - gate)
        gd = -gn * wkv
        an = scan_up(earlier(gn, back[0:1]), rate)
        ad = scan_up(earlier(gd, back[1:2]), rate)
        back[0:1] = gn[0:1] + fade * an[0:1]
        back[1:2] = gd[0:1] + fade * ad[0:1]
        now = b * (gn * v + gd)
        acc[10:11] += jnp.sum(now, axis=0, keepdims=True)
        acc[9:10] += jnp.sum(an * num + ad * den, axis=0, keepdims=True)
        gproj = (
            (e * (an * v + ad) + now).astype(BF),
            (b * gn + e * an).astype(BF),
            gr.astype(BF),
        )
        ready(0, 1, 2)
        grads = []
        for c in range(3):
            gst[slot, c * nt : (c + 1) * nt] = gproj[c]
            grads.append(dot(gproj[c], w[c]))
        gh = gmid + mix_back(
            grads, xh1[m].astype(F32), r1[m], car1[m, 0:1], gain[0:1], bias[0:1],
            (tmix[0:1], tmix[1:2], tmix[2:3]), 2, 0, 2, 4,
        )
        gbox[m] = gh.astype(BF)

        @pl.when(layer > 0)
        def _():
            remote(gbox.at[m], gbox.at[m], g_send.at[m], g_recv.at[m], bp, bi).start()

        @pl.when(layer == 0)
        def _():
            q = lax.div(m, per)
            u = m - q * per
            mine = jnp.logical_and(q == p, first + k == i)
            give(gbox.at[m], gb.at[pl.ds(pl.multiple_of(u * nt, nt), nt)], g_send.at[m], gb_recv.at[u], q, first + k, mine)

        local(gst.at[slot], go.at[m], go_sem.at[slot]).start()
        return none

    backward(0, 0, True)
    lax.fori_loop(1, nm, backward, 0)
    small[...] = acc[...]
    small[9:10] = acc[9:10] * (-rate * fade)

    for slot in range(min(2, nm)):
        drain(xst.at[slot], x_sem.at[slot])
        drain(gst.at[slot], go_sem.at[slot])

    def finish(m, none):
        drain(relu.at[m], relu_sem.at[m])
        mine = jnp.logical_and(lax.div(m, per) == p, first + k == i)

        @pl.when(jnp.logical_not(jnp.logical_and(layer == last, mine)))
        def _():
            drain(inbox.at[m], in_send.at[m])

        @pl.when(jnp.logical_not(jnp.logical_and(layer == 0, mine)))
        def _():
            drain(gbox.at[m], g_send.at[m])

        return none

    lax.fori_loop(0, nm, finish, 0)
    for u in range(per):
        part = pl.ds(u * nt, nt)
        drain(ob.at[part], ob_recv.at[u])
        drain(gb.at[part], gb_recv.at[u])

        @pl.when(jnp.logical_not(in_self))
        def _():
            drain(x_hbm.at[0, part], x0_send.at[u])

        @pl.when(jnp.logical_not(cot_self))
        def _():
            drain(cot_hbm.at[0, part], cot_send.at[u])

    @pl.when(jnp.logical_not(st_self))
    def _():
        for a, (src, dst) in enumerate(states):
            drain(dst, st_send.at[a])

    @pl.when(jnp.logical_not(fin_self))
    def _():
        for a, (src, dst) in enumerate(finals):
            drain(src, fin_send.at[a])

    for a, (src, dst) in enumerate(finals):
        drain(dst, fin_recv.at[a])

    @pl.when(owner)
    def _():
        for a, (src, dst) in enumerate(weights):
            drain(dst, w_send.at[a])


def sums_kernel(
    npipe, ngroups, x_hbm, g_hbm, small, out, out_small,
    xb, gbuf, dws, xs, own, rx, rr, ag, xs_s, own_s, rx_s, rr_s, ag_s,
    x_sem, g_sem, ex_send, ex_recv, r_send, r_recv, a_send, a_recv, o_send, o_recv, small_send, small_recv,
):
    p, i, y, k, first, s, m_chip = position()
    j = lax.div(i, 2)
    sib = 2 * y + 1 - k
    nc, half, width = own.shape
    quarter = half // 2
    rows_c = 2 * half
    split = width // rows_c
    nm, nt = xb.shape[1:3]
    nq = x_hbm.shape[1] // nt - 6
    hops = (ngroups - 1 - j, j)
    dist = (j, ngroups - 1 - j)
    step_by = (-1, 1)
    dest = 2 * y + m_chip
    other = first + 1 - s

    barrier = pltpu.get_barrier_semaphore()
    for bp, bi in ((sib, i), (p, other), (sib, other)):
        pl.semaphore_signal(barrier, inc=1, device_id=(bp, bi), device_id_type=MESH)

    @pl.when(j > 0)
    def _():
        pl.semaphore_signal(barrier, inc=1, device_id=(p, i - 2), device_id_type=MESH)

    @pl.when(j < ngroups - 1)
    def _():
        pl.semaphore_signal(barrier, inc=1, device_id=(p, i + 2), device_id_type=MESH)

    def blocks(c):
        b = lax.div(c, split)
        xi = jnp.where(b < 4, b, jnp.where(b < 4 + nq, 4, jnp.where(b < 4 + 2 * nq, b - nq + 2, 5)))
        gi = jnp.where(b < 4 + nq, b, jnp.where(b < 4 + 2 * nq, 4 + nq, 5 + nq))
        return b, xi, gi

    def loads(c, slot):
        b, xi, gi = blocks(c)
        part = c - b * split
        cols = pl.ds(pl.multiple_of(part * rows_c, rows_c), rows_c)
        return (
            local(x_hbm.at[:, pl.ds(pl.multiple_of(xi * nt, nt), nt), cols], xb.at[slot], x_sem.at[slot]),
            local(g_hbm.at[:, pl.ds(pl.multiple_of(gi * nt, nt), nt)], gbuf.at[slot], g_sem.at[slot]),
        )

    for copy in loads(0, 0):
        copy.start()

    neighbours = 3 + jnp.where(j > 0, 1, 0) + jnp.where(j < ngroups - 1, 1, 0)
    pl.semaphore_wait(barrier, neighbours)

    def produce(c):
        slot = lax.rem(c, 2)

        @pl.when(c + 1 < nc)
        def _():
            for copy in loads(c + 1, 1 - slot):
                copy.start()

        for copy in loads(c, slot):
            copy.wait()
        b = lax.div(c, split)

        @pl.when(jnp.logical_and(b >= 4 + nq, b < 4 + 2 * nq))
        def _():
            r = xb[slot].astype(F32)
            xb[slot] = (r * r).astype(BF)

        dws[...] = lax.dot_general(
            xb[slot].reshape(nm * nt, rows_c), gbuf[slot].reshape(nm * nt, width), (((0,), (0,)), ((), ())),
            preferred_element_type=F32,
        )

        @pl.when(c >= 2)
        def _():
            drain(xs.at[slot], ex_send.at[slot])

        xs[slot] = dws[pl.ds(pl.multiple_of((1 - k) * half, half), half)].astype(BF)
        remote(xs.at[slot], rx.at[c], ex_send.at[slot], ex_recv.at[c], sib, i).start()
        own[c] = dws[pl.ds(pl.multiple_of(k * half, half), half)]

        @pl.when(c == 0)
        def _():
            n = small.shape[0]
            mine = jnp.where(k == 0, 1.0, 0.0)
            own_s[...] = jnp.zeros_like(own_s)
            xs_s[...] = jnp.zeros_like(xs_s)
            own_s[0:n] = small[...] * mine
            xs_s[0:n] = (small[...] * (1.0 - mine)).astype(BF)
            remote(xs_s, rx_s, small_send.at[0], ex_recv.at[nc], sib, i).start()

    def exchange(c):
        drain(rx.at[c], ex_recv.at[c])
        own[c] = own[c] + rx[c].astype(F32)

        @pl.when(c == 0)
        def _():
            drain(rx_s, ex_recv.at[nc])
            own_s[...] = own_s[...] + rx_s[...].astype(F32)

    def reduce(c, d):
        def one(value, rr_at, ag_at, send, recv):
            @pl.when(hops[d] == 0)
            def _():
                rr_at[...] = value().astype(BF)

            @pl.when(hops[d] > 0)
            def _():
                drain(rr_at, recv)

                @pl.when(dist[d] > 0)
                def _():
                    rr_at[...] = (value() + rr_at[...].astype(F32)).astype(BF)

                @pl.when(dist[d] == 0)
                def _():
                    ag_at[...] = (value() + rr_at[...].astype(F32)).astype(BF)

            @pl.when(dist[d] > 0)
            def _():
                remote(rr_at, rr_at, send, recv, p, i + 2 * step_by[d]).start()

            @pl.when(jnp.logical_and(dist[d] == 0, hops[d] == 0))
            def _():
                ag_at[...] = rr_at[...]

        one(lambda: own[c, d * quarter : (d + 1) * quarter], rr.at[d, c], ag.at[d, c], r_send.at[d], r_recv.at[d, c])

        @pl.when(c == 0)
        def _():
            n = rr_s.shape[1]
            one(lambda: own_s[d * n : (d + 1) * n], rr_s.at[d], ag_s.at[d], small_send.at[1 + d], r_recv.at[d, nc])

    def spread(c, d):
        def one(ag_at, to, forward_send, recv, local_send, far_send, out_recv):
            @pl.when(dist[d] > 0)
            def _():
                drain(ag_at, recv)

            @pl.when(hops[d] > 0)
            def _():
                remote(ag_at, ag_at, forward_send, recv, p, i - 2 * step_by[d]).start()

            remote(ag_at, to, far_send, out_recv, dest, other).start()

            @pl.when(p == dest)
            def _():
                local(ag_at, to, out_recv).start()

            @pl.when(p != dest)
            def _():
                remote(ag_at, to, local_send, out_recv, dest, i).start()

        b = lax.div(c, split)
        row = (c - b * split) * rows_c + k * half + d * quarter
        to = out.at[b, pl.ds(pl.multiple_of(row, quarter), quarter)]
        one(ag.at[d, c], to, a_send.at[d], a_recv.at[d, c], o_send.at[0], o_send.at[1], o_recv.at[0])

        @pl.when(c == 0)
        def _():
            n = rr_s.shape[1]
            to_s = out_small.at[pl.ds(pl.multiple_of(k * 2 * n + d * n, n), n)]
            one(ag_s.at[d], to_s, small_send.at[3 + d], a_recv.at[d, nc], small_send.at[5 + d], small_send.at[7 + d], small_recv.at[0])

    def inside(c, f):
        @pl.when(jnp.logical_and(c >= 0, c < nc))
        def _():
            f(c)

    def step(t, none):
        inside(t, produce)
        inside(t - 1, exchange)
        for d in range(2):
            inside(t - 1 - LAG * hops[d], lambda c: reduce(c, d))
        for d in range(2):
            inside(t - 1 - LAG * (ngroups - 1 + dist[d]), lambda c: spread(c, d))
        return none

    lax.fori_loop(0, nc + 1 + 2 * LAG * (ngroups - 1), step, 0)

    for slot in range(min(2, nc)):
        drain(xs.at[slot], ex_send.at[slot])
    drain(xs_s, small_send.at[0])
    for d in range(2):

        @pl.when(dist[d] > 0)
        def _():
            drain(rr.at[d], r_send.at[d])
            drain(rr_s.at[d], small_send.at[1 + d])

        @pl.when(hops[d] > 0)
        def _():
            drain(ag.at[d], a_send.at[d])
            drain(ag_s.at[d], small_send.at[3 + d])

        @pl.when(p != dest)
        def _():
            drain(ag_s.at[d], small_send.at[5 + d])

        drain(ag_s.at[d], small_send.at[7 + d])

    @pl.when(p != dest)
    def _():
        drain(ag, o_send.at[0])

    drain(ag, o_send.at[1])
    drain(out, o_recv.at[0])
    drain(out_small, small_recv.at[0])


def widen_kernel(
    ob, gb, rows, w_in, w_out, w_key, w_val, w_rec,
    out, grad, gain, bias, tmix, cmix, decay, bonus, g_in, g_out, g_key, g_val, g_rec,
):
    for src, dst in ((ob, out), (gb, grad), (w_in, g_in), (w_out, g_out), (w_val, g_val), (w_rec, g_rec)):
        dst[...] = src[...].astype(F32)
    nq, _, width = w_key.shape
    for q in range(nq):
        g_key[:, q * width : (q + 1) * width] = w_key[q].astype(F32)
    at = 0
    for dst in (gain, bias, tmix, cmix, decay, bonus):
        dst[...] = rows[at : at + dst.shape[0]].astype(F32)
        at += dst.shape[0]


def body(
    block_input, ln_gain, ln_bias, tm_mix, cm_mix, time_decay, time_first, tm_in, tm_out,
    cm_key, cm_value, cm_recept, wkv_num, wkv_den, last_rows, cotangent,
):
    npipe, ndp = lax.axis_size("pipe"), lax.axis_size("dp")
    seg, width = block_input.shape[1:]
    hidden = cm_key.shape[2]
    nq = hidden // width
    length = seg * npipe
    nt = min(TOKENS, seg)
    nm, per = length // nt, seg // nt
    anywhere = pl.BlockSpec(memory_space=pl.ANY)
    vmem = pl.BlockSpec(memory_space=pltpu.VMEM)
    dma = pltpu.SemaphoreType.DMA
    shape = jax.ShapeDtypeStruct
    nb = 6 + nq
    nblocks = 5 + 2 * nq
    xs, gs, small, fin_num, fin_den, fin_rows, ob, gb, turned = pl.pallas_call(
        functools.partial(layers_kernel, npipe),
        name="layers",
        out_shape=[
            shape((nm, nb * nt, width), BF),
            shape((nm, nb * nt, width), BF),
            shape((16, width), F32),
            shape((1, 1, width), F32),
            shape((1, 1, width), F32),
            shape((1, 2, 1, width), F32),
            shape((seg, width), BF),
            shape((seg, width), BF),
            shape((nblocks, width, width), BF),
        ],
        in_specs=[anywhere] * 16,
        out_specs=[anywhere, anywhere, vmem] + [anywhere] * 6,
        scratch_shapes=[
            pltpu.VMEM((nblocks, width, width), BF),
            pltpu.VMEM((2, width), F32),
            pltpu.VMEM((2, width), F32),
            pltpu.VMEM((3, width), F32),
            pltpu.VMEM((2, width), F32),
            pltpu.VMEM((1, width), F32),
            pltpu.VMEM((1, width), F32),
            pltpu.VMEM((1, width), F32),
            pltpu.VMEM((1, width), F32),
            pltpu.VMEM((2, width), F32),
            pltpu.VMEM((nm, nt, width), BF),
            pltpu.VMEM((nm, nt, width), BF),
            *[pltpu.VMEM((nm, nt, width), F32)] * 4,
            *[pltpu.VMEM((nm, nt, width), BF)] * 5,
            pltpu.VMEM((nm, nq * nt, width), BF),
            *[pltpu.VMEM((nm, nt, 1), F32)] * 2,
            *[pltpu.VMEM((nm, 8, width), F32)] * 2,
            pltpu.VMEM((8, width), F32),
            pltpu.VMEM((16, width), F32),
            pltpu.VMEM((2, 6 * nt, width), BF),
            pltpu.VMEM((2, nb * nt, width), BF),
            dma((6 + nblocks,)), dma((6 + nblocks,)), dma((nm,)), dma((nm,)), dma((nm,)), dma((nm,)),
            dma((per,)), dma((per,)), dma((per,)), dma((per,)),
            dma((3,)), dma((3,)), dma((3,)), dma((3,)), dma((2,)), dma((2,)), dma((nm,)), dma((2,)), dma((nblocks,)),
        ],
        compiler_params=pltpu.CompilerParams(collective_id=0, has_side_effects=True, vmem_limit_bytes=VMEM_BYTES),
    )(block_input, cotangent, ln_gain, ln_bias, tm_mix, cm_mix, time_decay, time_first, wkv_num, wkv_den, last_rows,
      tm_in, tm_out, cm_key, cm_value, cm_recept)

    rows_c = width // SPLIT if width % (128 * SPLIT) == 0 else width // 2
    nc, half = nblocks * (width // rows_c), rows_c // 2
    quarter = half // 2
    out, out_small = pl.pallas_call(
        functools.partial(sums_kernel, npipe, ndp // 2),
        name="sums",
        out_shape=[shape((nblocks, width, width), BF), shape((64, width), BF)],
        in_specs=[anywhere, anywhere, vmem],
        out_specs=[anywhere, anywhere],
        scratch_shapes=[
            pltpu.VMEM((2, nm, nt, rows_c), BF),
            pltpu.VMEM((2, nm, nt, width), BF),
            pltpu.VMEM((rows_c, width), F32),
            pltpu.VMEM((2, half, width), BF),
            pltpu.VMEM((nc, half, width), F32),
            pltpu.VMEM((nc, half, width), BF),
            pltpu.VMEM((2, nc, quarter, width), BF),
            pltpu.VMEM((2, nc, quarter, width), BF),
            pltpu.VMEM((32, width), BF),
            pltpu.VMEM((32, width), F32),
            pltpu.VMEM((32, width), BF),
            pltpu.VMEM((2, 16, width), BF),
            pltpu.VMEM((2, 16, width), BF),
            dma((2,)), dma((2,)), dma((2,)), dma((nc + 1,)), dma((2,)), dma((2, nc + 1)), dma((2,)), dma((2, nc + 1)),
            dma((2,)), dma((1,)), dma((9,)), dma((1,)),
        ],
        compiler_params=pltpu.CompilerParams(collective_id=1, has_side_effects=True, vmem_limit_bytes=VMEM_BYTES),
    )(xs, gs, small)

    cuts = 16 if width % 256 == 0 else 2
    step = width // cuts

    def whole(*dims):
        return pl.BlockSpec(dims, lambda c: (0,) * len(dims))

    def part(rows, columns=width):
        return pl.BlockSpec((rows, columns), lambda c: (c, 0))

    def blocks(count, at):
        return pl.BlockSpec((count, step, width), lambda c: (at // count, c, 0))

    wide = pl.pallas_call(
        widen_kernel,
        name="widen",
        grid=(cuts,),
        out_shape=[
            shape((seg, width), F32), shape((seg, width), F32), shape((2, width), F32), shape((2, width), F32),
            shape((3, width), F32), shape((2, width), F32), shape((1, width), F32), shape((1, width), F32),
            shape((3, width, width), F32), shape((1, width, width), F32), shape((width, hidden), F32),
            shape((nq, width, width), F32), shape((1, width, width), F32),
        ],
        in_specs=[
            part(seg // cuts), part(seg // cuts), whole(64, width), blocks(3, 0), blocks(1, 3), blocks(nq, 4),
            blocks(nq, 4 + nq), blocks(1, 4 + 2 * nq),
        ],
        out_specs=[
            part(seg // cuts), part(seg // cuts), whole(2, width), whole(2, width), whole(3, width), whole(2, width),
            whole(1, width), whole(1, width), blocks(3, 0), blocks(1, 0), part(step, hidden), blocks(nq, 0), blocks(1, 0),
        ],
    )(ob, gb, out_small, out, out, out, out, out)
    return (
        wide[0][None],
        wide[1][None],
        wide[2][None],
        wide[3][None],
        wide[4][None],
        wide[5][None],
        wide[6],
        wide[7],
        wide[8][None],
        wide[9],
        wide[10][None],
        wide[11].reshape(1, hidden, width),
        wide[12],
        fin_num,
        fin_den,
        fin_rows,
    )


def solution(mesh):
    args = (
        P("dp", "pipe", None),
        P("pipe", None, None),
        P("pipe", None, None),
        P("pipe", None, None),
        P("pipe", None, None),
        P("pipe", None),
        P("pipe", None),
        P("pipe", None, None, None),
        P("pipe", None, None),
        P("pipe", None, None),
        P("pipe", None, None),
        P("pipe", None, None),
        P("pipe", "dp", None),
        P("pipe", "dp", None),
        P("pipe", None, "dp", None),
        P("dp", "pipe", None),
    )
    outs = (
        P("dp", "pipe", None),
        P("dp", "pipe", None),
        P("pipe", None, None),
        P("pipe", None, None),
        P("pipe", None, None),
        P("pipe", None, None),
        P("pipe", None),
        P("pipe", None),
        P("pipe", None, None, None),
        P("pipe", None, None),
        P("pipe", None, None),
        P("pipe", None, None),
        P("pipe", None, None),
        P("pipe", "dp", None),
        P("pipe", "dp", None),
        P("pipe", None, "dp", None),
    )
    return jax.shard_map(body, mesh=mesh, in_specs=args, out_specs=outs, check_vma=False)
```

profile of v0, /device:TPU:9, one launch (start us, length us, event | category | flops | bytes accessed | tf_op | source)
XLA Modules:
  0.0 380.4 jit_solution(8071654133811301102)
XLA Ops:
  0.6 1.3 copy.32.tmix_hbm
  1.9 158.2 %layers.1 = (bf16[8,1280,768]{2,1,0:T(8,128)(2,1)}, bf16[8,1280,768]{2,1,0:T(8,128)(2,1)}, f32[16,768]{1,0:T(8,128)}, f32[1,1,768]{2,1,0:T(1,128)}, f32[1,1,768]...) custom-call(bf16[1,256,768]{2,1,0:T(8,128)(2,1)} %x_hbm.1, ...), custom_call_target="tpu_custom_call" | custom-call | tf_op jit(solution)/shard_map/layers/pallas_call | solution.py:732
  160.2 197.9 %sums.1 = (bf16[13,768,768]{2,1,0:T(8,128)(2,1)}, bf16[64,768]{1,0:T(8,128)(2,1)}) custom-call(bf16[8,1280,768]{2,1,0:T(8,128)(2,1)} %get-tuple-element.41.x_hbm, bf16[8,1280,768]{2,1,0:T(8,128)(2,1)} %get-tuple-element.42.g_hbm, f32[16,768]{1,0:T(8,128)} %get-tuple-element.43.small), custom_call_target="tpu_custom_call" | custom-call | tf_op jit(solution)/shard_map/sums/pallas_call | solution.py:781
  358.1 0.0 copy-start.2
  358.1 0.0 copy-start.1
  358.1 0.0 copy-start
  358.1 19.3 %widen.1 = (f32[256,768]{1,0:T(8,128)}, f32[256,768]{1,0:T(8,128)}, f32[2,768]{1,0:T(2,128)}, f32[2,768]{1,0:T(2,128)}, f32[3,768]{1,0:T(4,128)}, /*index=5*/f32...) custom-call(bf16[256,768]{1,0:T(8,128)(2,1)} %get-tuple-element.39.o, ...), custom_call_target="tpu_custom_call" | custom-call | tf_op jit(solution)/shard_map/widen/pallas_call | solution.py:819
  377.4 1.3 copy.33
  378.7 0.0 copy-done.2
  378.7 0.6 copy.37
  379.3 0.0 copy-done.1
  379.3 0.6 copy.38
  379.8 0.0 copy-done
  379.8 0.6 copy.39
Async XLA Ops:
  358.1 20.6 %copy-start.2 = (f32[1,1,768]{2,1,0:T(1,128)S(1)}, f32[1,1,768]{2,1,0:T(1,128)}, u32[]{:S(2)}) copy-start(f32[1,1,768]{2,1,0:T(1,128)} %get-tuple-element.107) | copy-start | bytes 9220
  358.1 21.2 %copy-start.1 = (f32[1,1,768]{2,1,0:T(1,128)S(1)}, f32[1,1,768]{2,1,0:T(1,128)}, u32[]{:S(2)}) copy-start(f32[1,1,768]{2,1,0:T(1,128)} %get-tuple-element.108) | copy-start | bytes 9220
  358.1 21.7 %copy-start = (f32[1,2,1,768]{3,2,1,0:T(1,128)S(1)}, f32[1,2,1,768]{3,2,1,0:T(1,128)}, u32[]{:S(2)}) copy-start(f32[1,2,1,768]{3,2,1,0:T(1,128)} %get-tuple-element.109) | copy-start | bytes 18436
where the time goes:
time: 381 us; the launch traced here: 380 us
  Pallas kernels  375 us (98%)
  local copies, waits for them, and re-layouts  4.38 us (1%)
    pallas_call x1, Pallas kernels, body(): pl.pallas_call(functools.partial(sums_kernel, npipe, ndp // 2), name='sum...  198 us
    pallas_call x1, Pallas kernels, body(): pl.pallas_call(functools.partial(layers_kernel, npipe), name='layers', ou...  158 us
    pallas_call x1, Pallas kernels, body(): pl.pallas_call(widen_kernel, name='widen', grid=(cuts,), out_shape=[shape...  19.3 us

commit v1 on v0

--- a/solution.py
+++ b/solution.py
@@ -7,12 +7,16 @@
 from jax.experimental.pallas import tpu as pltpu
 from jax.sharding import PartitionSpec as P
 
+ON_CHIP = pltpu.VMEM
 MESH = pl.DeviceIdType.MESH
 BF, F32 = jnp.bfloat16, jnp.float32
 TOKENS = 128
+ROWS = 16
 SPLIT = 3
 LAG = 2
 VMEM_BYTES = 62 * 1024 * 1024
+SUMS_BYTES = 46 * 1024 * 1024
+WIDEN_BYTES = 16 * 1024 * 1024
 
 
 def position():
@@ -62,30 +66,29 @@
     return jnp.where(at == n - 1, row, pltpu.roll(v, n - 1, 0))
 
 
-def scan_down(v, rate):
-    n, by = v.shape[0], 1
-    while by < n:
+def fade_tables(table, rate):
+    at = lax.broadcasted_iota(jnp.int32, table.shape[1:], 0)
+    for n, by in enumerate((1, 2, 4)):
         fade = jnp.exp(-float(by) * rate)
-        if by < 8:
-            at = lax.broadcasted_iota(jnp.int32, v.shape, 0)
-            v = v + jnp.where(at >= by, fade * pltpu.roll(v, by, 0), 0.0)
-        else:
-            v = jnp.concatenate([v[:by], v[by:] + fade * v[: n - by]], axis=0)
-        by *= 2
-    return v
-
-
-def scan_up(v, rate):
-    n, by = v.shape[0], 1
-    while by < n:
-        fade = jnp.exp(-float(by) * rate)
-        if by < 8:
-            at = lax.broadcasted_iota(jnp.int32, v.shape, 0)
-            v = v + jnp.where(at < n - by, fade * pltpu.roll(v, n - by, 0), 0.0)
-        else:
-            v = jnp.concatenate([v[: n - by] + fade * v[by:], v[n - by :]], axis=0)
-        by *= 2
-    return v
+        table[n] = jnp.where(at >= by, fade, 0.0)
+        table[4 + n] = jnp.where(at < 8 - by, fade, 0.0)
+    far = at.astype(F32)
+    table[3] = jnp.exp(-(far + 1.0) * rate)
+    table[7] = jnp.exp(-(8.0 - far) * rate)
+
+
+def sums_before(v, carry, table):
+    for n, by in enumerate((1, 2, 4)):
+        v = v + table[n] * pltpu.roll(v, by, 0)
+    v = v + table[3] * carry
+    return later(v, carry), v[7:8]
+
+
+def sums_behind(v, carry, table):
+    for n, by in enumerate((1, 2, 4)):
+        v = v + table[4 + n] * pltpu.roll(v, 8 - by, 0)
+    v = v + table[7] * carry
+    return earlier(v, carry), v[0:1]
 
 
 def centred(v):
@@ -100,7 +103,7 @@
     win_hbm, wout_hbm, wck_hbm, wcv_hbm, wcr_hbm,
     xo, go, small, fin_num, fin_den, fin_rows, ob, gb, turned,
     w, gain, bias, tmix, cmix, decay, bonus_s, num_s, den_s, rows_s, inbox, gbox,
-    e_s, v_s, n_s, d_s, s_s, xh1, xh2, s2_s, c2_s, relu, r1, r2, car1, car2, back, acc, xst, gst,
+    e_s, v_s, n_s, d_s, s_s, xh1, xh2, s2_s, c2_s, relu, r1, r2, car1, car2, back, acc, xst, gst, table, t0, t1, t2, t3,
     w_send, w_recv, in_send, in_recv, g_send, g_recv, x0_send, cot_send, ob_recv, gb_recv,
     st_send, st_recv, fin_send, fin_recv, x_sem, go_sem, relu_sem, turn_out, turn_in,
 ):
@@ -113,7 +116,7 @@
     nblocks = w.shape[0]
     key, val, rec = 4, 4 + nq, 4 + 2 * nq
 
-    weights = [(gain_hbm.at[0], gain), (bias_hbm.at[0], bias), (tmix_hbm.at[0], tmix), (cmix_hbm.at[0], cmix),
+    weights = [(gain_hbm.at[0], gain), (bias_hbm.at[0], bias), (tmix_hbm, tmix), (cmix_hbm.at[0], cmix),
                (decay_hbm, decay), (first_hbm, bonus_s)]
     base = len(weights)
     order = [0, 1, 2, 3] + [at for q in range(nq) for at in (key + q, val + q)] + [rec]
@@ -184,6 +187,9 @@
     rate = jnp.exp(decay[...])
     bonus = jnp.exp(bonus_s[...])
     fade = jnp.exp(-rate)
+    fade_tables(table, rate)
+    tmixes = [tmix[c] for c in range(3)]
+    cmixes = [cmix[c : c + 1] for c in range(2)]
 
     @pl.when(layer == last)
     def _():
@@ -223,66 +229,77 @@
                 drain(xst.at[slot], x_sem.at[slot])
 
         drain(inbox.at[m], in_recv.at[m])
-        h = inbox[m].astype(F32)
-        xh, rs = centred(h)
-        xh1[m] = xh.astype(BF)
-        r1[m] = rs
-        xn = xh * gain[0:1] + bias[0:1]
-        prev = rows_s[0:1]
-        car1[m, 0:1] = prev
-        xp = later(xn, prev)
-        rows_s[0:1] = xn[nt - 1 :]
-        d = xn - xp
-        proj = []
-        for c in range(3):
-            mixed = (xp + tmix[c : c + 1] * d).astype(BF)
-            xst[slot, c * nt : (c + 1) * nt] = mixed
-            ready(c)
-            proj.append(dot(mixed, w[c]))
-        e = jnp.exp(proj[0])
-        v = proj[1]
-        ev = e * v
-        num = scan_down(later(ev, num_s[...]), rate)
-        den = scan_down(later(e, den_s[...]), rate)
-        num_s[...] = fade * num[nt - 1 :] + ev[nt - 1 :]
-        den_s[...] = fade * den[nt - 1 :] + e[nt - 1 :]
-        e_s[m] = e
-        v_s[m] = v
-        n_s[m] = num
-        d_s[m] = den
-        b = bonus * e
-        gate = jax.nn.sigmoid(proj[2])
-        s_s[m] = gate.astype(BF)
-        gated = (gate * ((num + b * v) / (den + b))).astype(BF)
-        xst[slot, 3 * nt : 4 * nt] = gated
+        def norm_mix(rows_of, which, xh_s, r_s, car, mixes, to):
+            before = rows_s[which : which + 1]
+            car[m, 0:1] = before
+            for r in range(0, nt, ROWS):
+                here = slice(r, r + ROWS)
+                xh, rs = centred(rows_of(here))
+                xh_s[m, here] = xh.astype(BF)
+                r_s[m, here] = rs
+                xn = xh * gain[which : which + 1] + bias[which : which + 1]
+                xp = later(xn, before)
+                before = xn[ROWS - 1 :]
+                d = xn - xp
+                for c, mix in enumerate(mixes):
+                    xst[slot, (to + c) * nt + r : (to + c) * nt + r + ROWS] = (xp + mix * d).astype(BF)
+            rows_s[which : which + 1] = before
+
+        norm_mix(lambda here: inbox[m, here].astype(F32), 0, xh1, r1, car1, tmixes, 0)
+        ready(0)
+        t0[...] = dot(xst[slot, 0:nt], w[0])
+        ready(1)
+        v_s[m] = dot(xst[slot, nt : 2 * nt], w[1])
+        ready(2)
+        t2[...] = dot(xst[slot, 2 * nt : 3 * nt], w[2])
+        nc, dc = num_s[...], den_s[...]
+        for r in range(0, nt, ROWS):
+            here = slice(r, r + ROWS)
+            gate = jax.nn.sigmoid(t2[here])
+            s_s[m, here] = gate.astype(BF)
+            wkv = []
+            for r8 in range(r, r + ROWS, 8):
+                rows = slice(r8, r8 + 8)
+                e = jnp.exp(t0[rows])
+                v = v_s[m, rows]
+                num, nc = sums_before(e * v, nc, table)
+                den, dc = sums_before(e, dc, table)
+                e_s[m, rows] = e
+                n_s[m, rows] = num
+                d_s[m, rows] = den
+                b = bonus * e
+                wkv.append((num + b * v) / (den + b))
+            xst[slot, 3 * nt + r : 3 * nt + r + ROWS] = (gate * jnp.concatenate(wkv, axis=0)).astype(BF)
+        num_s[...] = nc
+        den_s[...] = dc
         ready(3)
-        mid = h + dot(gated, w[3])
-        xh, rs = centred(mid)
-        xh2[m] = xh.astype(BF)
-        r2[m] = rs
-        xn = xh * gain[1:2] + bias[1:2]
-        prev = rows_s[1:2]
-        car2[m, 0:1] = prev
-        xp = later(xn, prev)
-        rows_s[1:2] = xn[nt - 1 :]
-        d = xn - xp
-        mixed0 = (xp + cmix[0:1] * d).astype(BF)
-        mixed1 = (xp + cmix[1:2] * d).astype(BF)
-        xst[slot, 4 * nt : 5 * nt] = mixed0
-        xst[slot, 5 * nt : 6 * nt] = mixed1
-        out = None
+        t1[...] = dot(xst[slot, 3 * nt : 4 * nt], w[3])
+
+        def middle(here):
+            mid = inbox[m, here].astype(F32) + t1[here]
+            t1[here] = mid
+            return mid
+
+        norm_mix(middle, 1, xh2, r2, car2, cmixes, 4)
+        squares = []
         for q in range(nq):
             ready(key + q)
-            r = jnp.maximum(dot(mixed0, w[key + q]), 0.0)
+            r = jnp.maximum(dot(xst[slot, 4 * nt : 5 * nt], w[key + q]), 0.0)
             relu[m, q * nt : (q + 1) * nt] = r.astype(BF)
+            squares.append((r * r).astype(BF))
+        ready(rec)
+        t2[...] = dot(xst[slot, 5 * nt : 6 * nt], w[rec])
+        for q in range(nq):
             ready(val + q)
-            part = dot((r * r).astype(BF), w[val + q])
-            out = part if out is None else out + part
-        ready(rec)
-        gate = jax.nn.sigmoid(dot(mixed1, w[rec]))
-        s2_s[m] = gate.astype(BF)
-        c2_s[m] = (out * gate * (1.0 - gate)).astype(BF)
-        inbox[m] = (mid + gate * out).astype(BF)
+        t0[...] = dot(jnp.concatenate(squares, axis=1), w[val : val + nq].reshape(nq * width, width))
+        for r in range(0, nt, ROWS):
+            here = slice(r, r + ROWS)
+            gate = jax.nn.sigmoid(t2[here])
+            out = t0[here]
+            s2_s[m, here] = gate.astype(BF)
+            gated = gate * out
+            c2_s[m, here] = (gated * (1.0 - gate)).astype(BF)
+            inbox[m, here] = (t1[here] + gated).astype(BF)
 
         @pl.when(layer < last)
         def _():
@@ -326,21 +343,38 @@
     back[...] = jnp.zeros_like(back)
     acc[...] = jnp.zeros_like(acc)
 
-    def mix_back(grads, xh, rs, prev, gain_row, bias_row, mixes, back_at, acc_gain, acc_bias, acc_mix):
-        xn = xh * gain_row + bias_row
-        d = xn - later(xn, prev)
-        here, total = None, None
-        for at, (g, mix) in enumerate(zip(grads, mixes)):
-            acc[acc_mix + at : acc_mix + at + 1] += jnp.sum(g * d, axis=0, keepdims=True)
-            here = g * mix if here is None else here + g * mix
-            total = g if total is None else total + g
-        shifted = total - here
-        gx = here + earlier(shifted, back[back_at : back_at + 1])
-        back[back_at : back_at + 1] = shifted[0:1]
-        acc[acc_gain : acc_gain + 1] += jnp.sum(gx * xh, axis=0, keepdims=True)
-        acc[acc_bias : acc_bias + 1] += jnp.sum(gx, axis=0, keepdims=True)
-        gp = gx * gain_row
-        return rs * (gp - jnp.mean(gp, axis=-1, keepdims=True) - xh * jnp.mean(gp * xh, axis=-1, keepdims=True))
+    def note(at, v):
+        acc[at] += v[0:8] + v[8:16]
+
+    def mix_back(m, parts, xh_s, r_s, car, which, mixes, rows_of, put, back_at, acc_mix):
+        gain_row, bias_row = gain[which : which + 1], bias[which : which + 1]
+        behind = back[back_at : back_at + 1]
+        for r in reversed(range(0, nt, ROWS)):
+            here = slice(r, r + ROWS)
+            xh = xh_s[m, here].astype(F32)
+            xn = xh * gain_row + bias_row
+            if r == 0:
+                before = car[m, 0:1]
+            else:
+                before = xh_s[m, r - ROWS : r].astype(F32)[ROWS - 1 :] * gain_row + bias_row
+            d = xn - later(xn, before)
+            own, total = None, None
+            for c, part in enumerate(parts):
+                g = part[here]
+                note(acc_mix + c, g * d)
+                mixed = g * mixes[c]
+                own = mixed if own is None else own + mixed
+                total = g if total is None else total + g
+            shifted = total - own
+            gx = own + earlier(shifted, behind)
+            behind = shifted[0:1]
+            note(which, gx * xh)
+            note(2 + which, gx)
+            gp = gx * gain_row
+            centre = jnp.mean(gp, axis=-1, keepdims=True)
+            slope = jnp.mean(gp * xh, axis=-1, keepdims=True)
+            put(here, rows_of(here) + r_s[m, here] * (gp - centre - xh * slope))
+        back[back_at : back_at + 1] = behind
 
     def backward(step, none, begin=False):
         m = nm - 1 - step
@@ -361,59 +395,68 @@
                 drain(gst.at[slot], go_sem.at[slot])
 
         drain(gbox.at[m], g_recv.at[m])
-        g = gbox[m].astype(F32)
-        gvo = (g * s2_s[m].astype(F32)).astype(BF)
-        grp = (g * c2_s[m].astype(F32)).astype(BF)
-        gst[slot, (4 + nq) * nt : (5 + nq) * nt] = gvo
-        gst[slot, (5 + nq) * nt : (6 + nq) * nt] = grp
-        gm0 = None
+        for r in range(0, nt, ROWS):
+            here = slice(r, r + ROWS)
+            g = gbox[m, here].astype(F32)
+            gst[slot, (4 + nq) * nt + r : (4 + nq) * nt + r + ROWS] = (g * s2_s[m, here].astype(F32)).astype(BF)
+            gst[slot, (5 + nq) * nt + r : (5 + nq) * nt + r + ROWS] = (g * c2_s[m, here].astype(F32)).astype(BF)
+        keys = []
         for q in range(nq):
             ready(val + q)
-            gs = dot(gvo, w[val + q])
-            gk = (gs * (2.0 * relu[m, q * nt : (q + 1) * nt].astype(F32))).astype(BF)
+            gs = dot(gst[slot, (4 + nq) * nt : (5 + nq) * nt], w[val + q]).astype(BF)
+            r = relu[m, q * nt : (q + 1) * nt]
+            gk = gs * (r + r)
             gst[slot, (4 + q) * nt : (5 + q) * nt] = gk
+            keys.append(gk)
+        ready(rec)
+        t1[...] = dot(gst[slot, (5 + nq) * nt : (6 + nq) * nt], w[rec])
+        for q in range(nq):
             ready(key + q)
-            part = dot(gk, w[key + q])
-            gm0 = part if gm0 is None else gm0 + part
-        ready(rec)
-        gm1 = dot(grp, w[rec])
-        gmid = g + mix_back(
-            (gm0, gm1), xh2[m].astype(F32), r2[m], car2[m, 0:1], gain[1:2], bias[1:2], (cmix[0:1], cmix[1:2]), 3, 1, 3, 7
-        )
-        gbranch = gmid.astype(BF)
-        gst[slot, 3 * nt : 4 * nt] = gbranch
+        t0[...] = dot(jnp.concatenate(keys, axis=1), w[key : key + nq].reshape(nq * width, width))
+
+        def put_mid(here, v):
+            t3[here] = v
+            gst[slot, 3 * nt + here.start : 3 * nt + here.stop] = v.astype(BF)
+
+        mix_back(m, (t0, t1), xh2, r2, car2, 1, cmixes, lambda here: gbox[m, here].astype(F32), put_mid, 3, 7)
         ready(3)
-        gg = dot(gbranch, w[3])
-        gate = s_s[m].astype(F32)
-        e, v, num, den = e_s[m], v_s[m], n_s[m], d_s[m]
-        b = bonus * e
-        inv = 1.0 / (den + b)
-        wkv = (num + b * v) * inv
-        gn = gg * gate * inv
-        gr = gg * wkv * gate * (1.0 - gate)
-        gd = -gn * wkv
-        an = scan_up(earlier(gn, back[0:1]), rate)
-        ad = scan_up(earlier(gd, back[1:2]), rate)
-        back[0:1] = gn[0:1] + fade * an[0:1]
-        back[1:2] = gd[0:1] + fade * ad[0:1]
-        now = b * (gn * v + gd)
-        acc[10:11] += jnp.sum(now, axis=0, keepdims=True)
-        acc[9:10] += jnp.sum(an * num + ad * den, axis=0, keepdims=True)
-        gproj = (
-            (e * (an * v + ad) + now).astype(BF),
-            (b * gn + e * an).astype(BF),
-            gr.astype(BF),
-        )
+        t0[...] = dot(gst[slot, 3 * nt : 4 * nt], w[3])
+        nc, dc = back[0:1], back[1:2]
+        for r in reversed(range(0, nt, ROWS)):
+            here = slice(r, r + ROWS)
+            gates = s_s[m, here].astype(F32)
+            outs = []
+            for r8 in (r + 8, r):
+                rows = slice(r8, r8 + 8)
+                gg = t0[rows]
+                gate = gates[r8 - r : r8 - r + 8]
+                e, v, num, den = e_s[m, rows], v_s[m, rows], n_s[m, rows], d_s[m, rows]
+                b = bonus * e
+                inv = 1.0 / (den + b)
+                wkv = (num + b * v) * inv
+                gw = gg * gate
+                gn = gw * inv
+                gr = gw * wkv * (1.0 - gate)
+                gd = -gn * wkv
+                an, nc = sums_behind(gn, nc, table)
+                ad, dc = sums_behind(gd, dc, table)
+                now = b * (gn * v + gd)
+                acc[10] += now
+                acc[9] += an * num + ad * den
+                outs.append((e * (an * v + ad) + now, b * gn + e * an, gr))
+            for c in range(3):
+                both = jnp.concatenate([outs[1][c], outs[0][c]], axis=0)
+                gst[slot, c * nt + r : c * nt + r + ROWS] = both.astype(BF)
+        back[0:1] = nc
+        back[1:2] = dc
         ready(0, 1, 2)
-        grads = []
-        for c in range(3):
-            gst[slot, c * nt : (c + 1) * nt] = gproj[c]
-            grads.append(dot(gproj[c], w[c]))
-        gh = gmid + mix_back(
-            grads, xh1[m].astype(F32), r1[m], car1[m, 0:1], gain[0:1], bias[0:1],
-            (tmix[0:1], tmix[1:2], tmix[2:3]), 2, 0, 2, 4,
-        )
-        gbox[m] = gh.astype(BF)
+        for c, t in enumerate((t0, t1, t2)):
+            t[...] = dot(gst[slot, c * nt : (c + 1) * nt], w[c])
+
+        def put_out(here, v):
+            gbox[m, here] = v.astype(BF)
+
+        mix_back(m, (t0, t1, t2), xh1, r1, car1, 0, tmixes, lambda here: t3[here], put_out, 2, 4)
 
         @pl.when(layer > 0)
         def _():
@@ -431,8 +474,9 @@
 
     backward(0, 0, True)
     lax.fori_loop(1, nm, backward, 0)
-    small[...] = acc[...]
-    small[9:10] = acc[9:10] * (-rate * fade)
+    for at in range(16):
+        row = jnp.sum(acc[at], axis=0, keepdims=True)
+        small[at : at + 1] = row * (-rate * fade) if at == 9 else row
 
     for slot in range(min(2, nm)):
         drain(xst.at[slot], x_sem.at[slot])
@@ -698,18 +742,67 @@
 
 
 def widen_kernel(
-    ob, gb, rows, w_in, w_out, w_key, w_val, w_rec,
-    out, grad, gain, bias, tmix, cmix, decay, bonus, g_in, g_out, g_key, g_val, g_rec,
+    ob, gb, rows, w, num, den, last,
+    out, grad, g_in, g_out, g_key, g_val, g_rec, gain, bias, tmix, cmix, decay, bonus, fin_num, fin_den, fin_rows,
+    stage, narrow, wide, sem, in_sem, out_sem,
 ):
-    for src, dst in ((ob, out), (gb, grad), (w_in, g_in), (w_out, g_out), (w_val, g_val), (w_rec, g_rec)):
-        dst[...] = src[...].astype(F32)
-    nq, _, width = w_key.shape
-    for q in range(nq):
-        g_key[:, q * width : (q + 1) * width] = w_key[q].astype(F32)
+    nblocks, width, _ = w.shape
+    slots, step, _ = stage.shape
+    nq, cuts = (nblocks - 5) // 2, width // step
+    for n, src in enumerate((ob, gb)):
+        local(src, narrow.at[n], in_sem.at[n]).start()
+
+    def one(t, none):
+        slot = lax.rem(t, slots)
+        b = lax.div(t, cuts)
+        cut = pl.ds(pl.multiple_of((t - b * cuts) * step, step), step)
+
+        @pl.when(t >= slots)
+        def _():
+            drain(stage.at[slot], sem.at[slot])
+
+        stage[slot] = w[b, cut].astype(F32)
+
+        @pl.when(b < 3)
+        def _():
+            local(stage.at[slot], g_in.at[b, cut], sem.at[slot]).start()
+
+        @pl.when(b == 3)
+        def _():
+            local(stage.at[slot], g_out.at[0, cut], sem.at[slot]).start()
+
+        for q in range(nq):
+
+            @pl.when(b == 4 + q)
+            def _():
+                local(stage.at[slot], g_key.at[cut, q * width : (q + 1) * width], sem.at[slot]).start()
+
+        @pl.when(jnp.logical_and(b >= 4 + nq, b < 4 + 2 * nq))
+        def _():
+            local(stage.at[slot], g_val.at[b - 4 - nq, cut], sem.at[slot]).start()
+
+        @pl.when(b == 4 + 2 * nq)
+        def _():
+            local(stage.at[slot], g_rec.at[0, cut], sem.at[slot]).start()
+
+        return none
+
+    lax.fori_loop(0, nblocks * cuts, one, 0)
+    for n, dst in enumerate((out, grad)):
+        drain(narrow.at[n], in_sem.at[n])
+        wide[n] = narrow[n].astype(F32)
+        local(wide.at[n], dst, out_sem.at[n]).start()
     at = 0
     for dst in (gain, bias, tmix, cmix, decay, bonus):
-        dst[...] = rows[at : at + dst.shape[0]].astype(F32)
-        at += dst.shape[0]
+        n = dst.shape[0]
+        dst[...] = rows[at : at + n].astype(F32).reshape(dst.shape)
+        at += n
+    for src, dst in ((num, fin_num), (den, fin_den), (last, fin_rows)):
+        dst[...] = src[...]
+    for slot in range(slots):
+        drain(stage.at[slot], sem.at[slot])
+    for n in range(2):
+        drain(wide.at[n], out_sem.at[n])
 
 
 def body(
@@ -749,7 +842,7 @@
             pltpu.VMEM((nblocks, width, width), BF),
             pltpu.VMEM((2, width), F32),
             pltpu.VMEM((2, width), F32),
-            pltpu.VMEM((3, width), F32),
+            pltpu.VMEM((3, 1, width), F32),
             pltpu.VMEM((2, width), F32),
             pltpu.VMEM((1, width), F32),
             pltpu.VMEM((1, width), F32),
@@ -764,15 +857,17 @@
             *[pltpu.VMEM((nm, nt, 1), F32)] * 2,
             *[pltpu.VMEM((nm, 8, width), F32)] * 2,
             pltpu.VMEM((8, width), F32),
-            pltpu.VMEM((16, width), F32),
+            pltpu.VMEM((16, 8, width), F32),
             pltpu.VMEM((2, 6 * nt, width), BF),
             pltpu.VMEM((2, nb * nt, width), BF),
+            pltpu.VMEM((8, 8, width), F32),
+            *[pltpu.VMEM((nt, width), F32)] * 4,
             dma((6 + nblocks,)), dma((6 + nblocks,)), dma((nm,)), dma((nm,)), dma((nm,)), dma((nm,)),
             dma((per,)), dma((per,)), dma((per,)), dma((per,)),
             dma((3,)), dma((3,)), dma((3,)), dma((3,)), dma((2,)), dma((2,)), dma((nm,)), dma((2,)), dma((nblocks,)),
         ],
         compiler_params=pltpu.CompilerParams(collective_id=0, has_side_effects=True, vmem_limit_bytes=VMEM_BYTES),
-    )(block_input, cotangent, ln_gain, ln_bias, tm_mix, cm_mix, time_decay, time_first, wkv_num, wkv_den, last_rows,
+    )(block_input, cotangent, ln_gain, ln_bias, jnp.swapaxes(tm_mix, 0, 1), cm_mix, time_decay, time_first, wkv_num, wkv_den, last_rows,
       tm_in, tm_out, cm_key, cm_value, cm_recept)
 
     rows_c = width // SPLIT if width % (128 * SPLIT) == 0 else width // 2
@@ -781,9 +876,9 @@
     out, out_small = pl.pallas_call(
         functools.partial(sums_kernel, npipe, ndp // 2),
         name="sums",
-        out_shape=[shape((nblocks, width, width), BF), shape((64, width), BF)],
+        out_shape=[ON_CHIP((nblocks, width, width), BF), ON_CHIP((64, width), BF)],
         in_specs=[anywhere, anywhere, vmem],
-        out_specs=[anywhere, anywhere],
+        out_specs=[vmem, vmem],
         scratch_shapes=[
             pltpu.VMEM((2, nm, nt, rows_c), BF),
             pltpu.VMEM((2, nm, nt, width), BF),
@@ -801,57 +896,47 @@
             dma((2,)), dma((2,)), dma((2,)), dma((nc + 1,)), dma((2,)), dma((2, nc + 1)), dma((2,)), dma((2, nc + 1)),
             dma((2,)), dma((1,)), dma((9,)), dma((1,)),
         ],
-        compiler_params=pltpu.CompilerParams(collective_id=1, has_side_effects=True, vmem_limit_bytes=VMEM_BYTES),
+        compiler_params=pltpu.CompilerParams(collective_id=1, has_side_effects=True, vmem_limit_bytes=SUMS_BYTES),
     )(xs, gs, small)
 
-    cuts = 16 if width % 256 == 0 else 2
-    step = width // cuts
-
-    def whole(*dims):
-        return pl.BlockSpec(dims, lambda c: (0,) * len(dims))
-
-    def part(rows, columns=width):
-        return pl.BlockSpec((rows, columns), lambda c: (c, 0))
-
-    def blocks(count, at):
-        return pl.BlockSpec((count, step, width), lambda c: (at // count, c, 0))
-
+    in_vmem = pltpu.with_memory_space_constraint(out, pltpu.VMEM)
     wide = pl.pallas_call(
         widen_kernel,
         name="widen",
-        grid=(cuts,),
         out_shape=[
-            shape((seg, width), F32), shape((seg, width), F32), shape((2, width), F32), shape((2, width), F32),
-            shape((3, width), F32), shape((2, width), F32), shape((1, width), F32), shape((1, width), F32),
-            shape((3, width, width), F32), shape((1, width, width), F32), shape((width, hidden), F32),
-            shape((nq, width, width), F32), shape((1, width, width), F32),
+            shape((seg, width), F32), shape((seg, width), F32), shape((3, width, width), F32), shape((1, width, width), F32),
+            shape((width, hidden), F32), shape((nq, width, width), F32), shape((1, width, width), F32),
+            shape((2, width), F32), shape((2, width), F32), shape((3, 1, width), F32), shape((2, width), F32),
+            shape((1, width), F32), shape((1, width), F32),
+            shape((1, 1, width), F32), shape((1, 1, width), F32), shape((1, 2, 1, width), F32),
         ],
-        in_specs=[
-            part(seg // cuts), part(seg // cuts), whole(64, width), blocks(3, 0), blocks(1, 3), blocks(nq, 4),
-            blocks(nq, 4 + nq), blocks(1, 4 + 2 * nq),
+        in_specs=[anywhere, anywhere, vmem, vmem, vmem, vmem, vmem],
+        out_specs=[anywhere] * 7 + [vmem] * 9,
+        scratch_shapes=[
+            pltpu.VMEM((4, width // 2, width), F32),
+            pltpu.VMEM((2, seg, width), BF),
+            pltpu.VMEM((2, seg, width), F32),
+            dma((4,)), dma((2,)), dma((2,)),
         ],
-        out_specs=[
-            part(seg // cuts), part(seg // cuts), whole(2, width), whole(2, width), whole(3, width), whole(2, width),
-            whole(1, width), whole(1, width), blocks(3, 0), blocks(1, 0), part(step, hidden), blocks(nq, 0), blocks(1, 0),
-        ],
-    )(ob, gb, out_small, out, out, out, out, out)
+        compiler_params=pltpu.CompilerParams(vmem_limit_bytes=WIDEN_BYTES),
+    )(ob, gb, out_small, in_vmem, fin_num, fin_den, fin_rows)
     return (
         wide[0][None],
         wide[1][None],
+        wide[7][None],
+        wide[8][None],
+        jnp.swapaxes(wide[9], 0, 1),
+        wide[10][None],
+        wide[11],
+        wide[12],
         wide[2][None],
-        wide[3][None],
+        wide[3],
         wide[4][None],
-        wide[5][None],
+        wide[5].reshape(1, hidden, width),
         wide[6],
-        wide[7],
-        wide[8][None],
-        wide[9],
-        wide[10][None],
-        wide[11].reshape(1, hidden, width),
-        wide[12],
-        fin_num,
-        fin_den,
-        fin_rows,
+        wide[13],
+        wide[14],
+        wide[15],
     )
 
 

time: 381 us -> 366 us (0.961)
  Pallas kernels: 375 us -> 365 us
  local copies, waits for them, and re-layouts: 4.38 us -> 0.02 us
    pallas_call x1, Pallas kernels: 19.3 us -> 11.7 us  [body(): pl.pallas_call(widen_kernel, name='widen', out_shape=[shape((seg, width),...]
    unnamed x11 -> x10, local copies, waits for them, and re-layouts: 4.38 us -> 0.02 us
where the time goes in v1:
time: 366 us
  Pallas kernels  365 us (100%)
    pallas_call x1, Pallas kernels, body(): pl.pallas_call(functools.partial(sums_kernel, npipe, ndp // 2), name='sum...  198 us
    pallas_call x1, Pallas kernels, body(): pl.pallas_call(functools.partial(layers_kernel, npipe), name='layers', ou...  155 us
    pallas_call x1, Pallas kernels, body(): pl.pallas_call(widen_kernel, name='widen', out_shape=[shape((seg, width),...  11.7 us

profile of v1, /device:TPU:9, one launch (start us, length us, event | category | flops | bytes accessed | tf_op | source)
XLA Modules:
  0.0 365.7 jit_solution(13979660141865226702)
XLA Ops:
  0.7 155.2 %layers.1 = (bf16[8,1280,768]{2,1,0:T(8,128)(2,1)}, bf16[8,1280,768]{2,1,0:T(8,128)(2,1)}, f32[16,768]{1,0:T(8,128)}, f32[1,1,768]{2,1,0:T(1,128)}, f32[1,1,768]...) custom-call(bf16[1,256,768]{2,1,0:T(8,128)(2,1)} %x_hbm.1, ...), custom_call_target="tpu_custom_call" | custom-call | tf_op jit(solution)/shard_map/layers/pallas_call | solution.py:825
  155.9 0.0 copy-start
  155.9 0.0 copy-start.1
  155.9 0.0 copy-start.2
  155.9 0.0 copy-start.3
  155.9 0.0 copy-start.4
  155.9 197.8 %sums.1 = (bf16[13,768,768]{2,1,0:T(8,128)(2,1)S(1)}, bf16[64,768]{1,0:T(8,128)(2,1)S(1)}) custom-call(bf16[8,1280,768]{2,1,0:T(8,128)(2,1)} %get-tuple-element.44.x_hbm, bf16[8,1280,768]{2,1,0:T(8,128)(2,1)} %get-tuple-element.45.g_hbm, f32[16,768]{1,0:T(8,128)} %get-tuple-element.46.small), custom_call_target="tpu_custom_call" | custom-call | tf_op jit(solution)/shard_map/sums/pallas_call | solution.py:876
  353.8 0.0 copy-done
  353.8 0.0 copy-done.1
  353.8 0.0 copy-done.2
  353.8 0.0 copy-done.3
  353.8 0.0 copy-done.4
  353.8 11.7 %widen.1 = (f32[256,768]{1,0:T(8,128)}, f32[256,768]{1,0:T(8,128)}, f32[3,768,768]{2,1,0:T(8,128)}, f32[1,768,768]{2,1,0:T(8,128)}, f32[768,3072]{1,0:T(8,128)},...) custom-call(bf16[256,768]{1,0:T(8,128)(2,1)S(1)} %copy-done, ...), custom_call_target="tpu_custom_call" | custom-call | tf_op jit(solution)/shard_map/widen/pallas_call | solution.py:903
Async XLA Ops:
  155.9 197.9 %copy-start = (bf16[256,768]{1,0:T(8,128)(2,1)S(1)}, bf16[256,768]{1,0:T(8,128)(2,1)}, u32[]{:S(2)}) copy-start(bf16[256,768]{1,0:T(8,128)(2,1)} %get-tuple-element.42.ob) | copy-start | bytes 1179652
  155.9 197.9 %copy-start.1 = (bf16[256,768]{1,0:T(8,128)(2,1)S(1)}, bf16[256,768]{1,0:T(8,128)(2,1)}, u32[]{:S(2)}) copy-start(bf16[256,768]{1,0:T(8,128)(2,1)} %get-tuple-element.43.gb) | copy-start | bytes 1179652
  155.9 197.9 %copy-start.2 = (f32[1,2,1,768]{3,2,1,0:T(1,128)S(1)}, f32[1,2,1,768]{3,2,1,0:T(1,128)}, u32[]{:S(2)}) copy-start(f32[1,2,1,768]{3,2,1,0:T(1,128)} %get-tuple-element.51.last) | copy-start | bytes 18436
  155.9 197.9 %copy-start.3 = (f32[1,1,768]{2,1,0:T(1,128)S(1)}, f32[1,1,768]{2,1,0:T(1,128)}, u32[]{:S(2)}) copy-start(f32[1,1,768]{2,1,0:T(1,128)} %get-tuple-element.49.num) | copy-start | bytes 9220
  155.9 197.9 %copy-start.4 = (f32[1,1,768]{2,1,0:T(1,128)S(1)}, f32[1,1,768]{2,1,0:T(1,128)}, u32[]{:S(2)}) copy-start(f32[1,1,768]{2,1,0:T(1,128)} %get-tuple-element.50.den) | copy-start | bytes 9220

commit v2 on v1

--- a/solution.py
+++ b/solution.py
@@ -14,8 +14,11 @@
 ROWS = 16
 SPLIT = 3
 LAG = 2
+GUESTS = 2
+GUEST_AT = 4
+GUEST_TURN = 20
 VMEM_BYTES = 62 * 1024 * 1024
-SUMS_BYTES = 46 * 1024 * 1024
+SUMS_BYTES = 47 * 1024 * 1024
 WIDEN_BYTES = 16 * 1024 * 1024
 
 
@@ -530,14 +533,19 @@
 
 
 def sums_kernel(
-    npipe, ngroups, x_hbm, g_hbm, small, out, out_small,
-    xb, gbuf, dws, xs, own, rx, rr, ag, xs_s, own_s, rx_s, rr_s, ag_s,
+    npipe, ngroups, guests, x_hbm, g_hbm, small, out, out_small,
+    xb, gbuf, dws, xs, own, rx, rr, ag, xs_s, own_s, rx_s, rr_s, ag_s, gx, gsrc,
     x_sem, g_sem, ex_send, ex_recv, r_send, r_recv, a_send, a_recv, o_send, o_recv, small_send, small_recv,
+    gx_send, gx_recv, guest_send, guest_ready,
 ):
     p, i, y, k, first, s, m_chip = position()
     j = lax.div(i, 2)
     sib = 2 * y + 1 - k
-    nc, half, width = own.shape
+    half, width = own.shape[1:]
+    nc = rx.shape[0]
+    low, high = GUEST_AT, GUEST_AT + guests
+    lower = y == 0
+    upper = y == 1
     quarter = half // 2
     rows_c = 2 * half
     split = width // rows_c
@@ -561,6 +569,25 @@
     def _():
         pl.semaphore_signal(barrier, inc=1, device_id=(p, i + 2), device_id_type=MESH)
 
+    greeted = 3 + jnp.where(j > 0, 1, 0) + jnp.where(j < ngroups - 1, 1, 0)
+    if guests:
+
+        @pl.when(upper)
+        def _():
+            for bp, bi in ((k, i), (s, first), (s, first + 1)):
+                pl.semaphore_signal(barrier, inc=1, device_id=(bp, bi), device_id_type=MESH)
+
+        greeted = greeted + jnp.where(lower, 3, 0)
+
+    def enter():
+        pl.semaphore_wait(barrier, greeted)
+        if guests:
+
+            @pl.when(lower)
+            def _():
+                for op in (2, 3):
+                    pl.semaphore_signal(guest_ready, inc=1, device_id=(op, first + k), device_id_type=MESH)
+
     def blocks(c):
         b = lax.div(c, split)
         xi = jnp.where(b < 4, b, jnp.where(b < 4 + nq, 4, jnp.where(b < 4 + 2 * nq, b - nq + 2, 5)))
@@ -579,9 +606,6 @@
     for copy in loads(0, 0):
         copy.start()
 
-    neighbours = 3 + jnp.where(j > 0, 1, 0) + jnp.where(j < ngroups - 1, 1, 0)
-    pl.semaphore_wait(barrier, neighbours)
-
     def produce(c):
         slot = lax.rem(c, 2)
 
@@ -607,6 +631,10 @@
         @pl.when(c >= 2)
         def _():
             drain(xs.at[slot], ex_send.at[slot])
+
+        @pl.when(c == 0)
+        def _():
+            enter()
 
         xs[slot] = dws[pl.ds(pl.multiple_of((1 - k) * half, half), half)].astype(BF)
         remote(xs.at[slot], rx.at[c], ex_send.at[slot], ex_recv.at[c], sib, i).start()
@@ -622,9 +650,23 @@
             xs_s[0:n] = (small[...] * (1.0 - mine)).astype(BF)
             remote(xs_s, rx_s, small_send.at[0], ex_recv.at[nc], sib, i).start()
 
+    def welcome(c):
+        @pl.when(c == nc)
+        def _():
+            pl.semaphore_wait(guest_ready, 2)
+
+        drain(gx.at[c - nc], gx_recv.at[c - nc])
+        own[c] = gx[c - nc].astype(F32)
+
     def exchange(c):
         drain(rx.at[c], ex_recv.at[c])
         own[c] = own[c] + rx[c].astype(F32)
+        if guests:
+
+            @pl.when(jnp.logical_and(lower, jnp.logical_and(c >= low, c < high)))
+            def _():
+                gsrc[c - low] = own[c].astype(BF)
+                remote(gsrc.at[c - low], gx.at[c - low], gx_send.at[0], gx_recv.at[c - low], p + 2, i).start()
 
         @pl.when(c == 0)
         def _():
@@ -662,18 +704,20 @@
         @pl.when(c == 0)
         def _():
             n = rr_s.shape[1]
-            one(lambda: own_s[d * n : (d + 1) * n], rr_s.at[d], ag_s.at[d], small_send.at[1 + d], r_recv.at[d, nc])
+            one(lambda: own_s[d * n : (d + 1) * n], rr_s.at[d], ag_s.at[d], small_send.at[1 + d], r_recv.at[d, nc + guests])
 
     def spread(c, d):
+        def come(ag_at, forward_send, recv):
+            @pl.when(dist[d] > 0)
+            def _():
+                drain(ag_at, recv)
+
+            @pl.when(hops[d] > 0)
+            def _():
+                remote(ag_at, ag_at, forward_send, recv, p, i - 2 * step_by[d]).start()
+
         def one(ag_at, to, forward_send, recv, local_send, far_send, out_recv):
-            @pl.when(dist[d] > 0)
-            def _():
-                drain(ag_at, recv)
-
-            @pl.when(hops[d] > 0)
-            def _():
-                remote(ag_at, ag_at, forward_send, recv, p, i - 2 * step_by[d]).start()
-
+            come(ag_at, forward_send, recv)
             remote(ag_at, to, far_send, out_recv, dest, other).start()
 
             @pl.when(p == dest)
@@ -684,32 +728,100 @@
             def _():
                 remote(ag_at, to, local_send, out_recv, dest, i).start()
 
-        b = lax.div(c, split)
-        row = (c - b * split) * rows_c + k * half + d * quarter
-        to = out.at[b, pl.ds(pl.multiple_of(row, quarter), quarter)]
-        one(ag.at[d, c], to, a_send.at[d], a_recv.at[d, c], o_send.at[0], o_send.at[1], o_recv.at[0])
+        def place(c):
+            b = lax.div(c, split)
+            row = (c - b * split) * rows_c + k * half + d * quarter
+            return out.at[b, pl.ds(pl.multiple_of(row, quarter), quarter)]
+
+        def own_chunk():
+            one(ag.at[d, c], place(c), a_send.at[d], a_recv.at[d, c], o_send.at[0], o_send.at[1], o_recv.at[0])
+
+        if guests:
+            pl.when(c < nc)(own_chunk)
+
+            @pl.when(c >= nc)
+            def _():
+                come(ag.at[d, c], a_send.at[d], a_recv.at[d, c])
+                to = place(c - nc + low)
+                remote(ag.at[d, c], to, guest_send.at[0], o_recv.at[0], s, i).start()
+                remote(ag.at[d, c], to, guest_send.at[1], o_recv.at[0], s, other).start()
+        else:
+            own_chunk()
 
         @pl.when(c == 0)
         def _():
             n = rr_s.shape[1]
             to_s = out_small.at[pl.ds(pl.multiple_of(k * 2 * n + d * n, n), n)]
-            one(ag_s.at[d], to_s, small_send.at[3 + d], a_recv.at[d, nc], small_send.at[5 + d], small_send.at[7 + d], small_recv.at[0])
-
-    def inside(c, f):
-        @pl.when(jnp.logical_and(c >= 0, c < nc))
-        def _():
-            f(c)
+            one(ag_s.at[d], to_s, small_send.at[3 + d], a_recv.at[d, nc + guests], small_send.at[5 + d], small_send.at[7 + d], small_recv.at[0])
+
+    def turn(u, own_work, guest_work=None):
+        if not guests:
+
+            @pl.when(jnp.logical_and(u >= 0, u < nc))
+            def _():
+                own_work(u)
+
+            return
+        at = min(GUEST_TURN, nc)
+        c = jnp.where(u < at, u, jnp.where(u < at + guests, nc + u - at, u - guests))
+        c = jnp.where(upper, c, u)
+        mine = jnp.logical_and(u >= 0, u < nc + jnp.where(upper, guests, 0))
+        if guest_work is not own_work:
+
+            @pl.when(jnp.logical_and(mine, c < nc))
+            def _():
+                own_work(c)
+
+            if guest_work is not None:
+
+                @pl.when(jnp.logical_and(mine, c >= nc))
+                def _():
+                    guest_work(c)
+
+        else:
+            away = jnp.logical_and(lower, jnp.logical_and(c >= low, c < high))
+
+            @pl.when(jnp.logical_and(mine, jnp.logical_not(away)))
+            def _():
+                own_work(c)
 
     def step(t, none):
-        inside(t, produce)
-        inside(t - 1, exchange)
+        turn(t, produce)
+        turn(t - 1, exchange, welcome)
         for d in range(2):
-            inside(t - 1 - LAG * hops[d], lambda c: reduce(c, d))
+            work = functools.partial(reduce, d=d)
+            turn(t - 1 - LAG * hops[d], work, work)
         for d in range(2):
-            inside(t - 1 - LAG * (ngroups - 1 + dist[d]), lambda c: spread(c, d))
+            work = functools.partial(spread, d=d)
+            turn(t - 1 - LAG * (ngroups - 1 + dist[d]), work, work)
         return none
 
-    lax.fori_loop(0, nc + 1 + 2 * LAG * (ngroups - 1), step, 0)
+    lax.fori_loop(0, nc + guests + 1 + 2 * LAG * (ngroups - 1), step, 0)
+
+    def settle(ref, sem):
+        if not guests:
+            drain(ref, sem)
+            return
+
+        @pl.when(upper)
+        def _():
+            drain(ref, sem)
+
+        @pl.when(lower)
+        def _():
+            drain(ref.at[pl.ds(0, low)], sem)
+            drain(ref.at[pl.ds(high, nc - high)], sem)
+
+    def settle_own(ref, sem):
+        if not guests:
+            drain(ref, sem)
+            return
+        drain(ref.at[pl.ds(0, low)], sem)
+        drain(ref.at[pl.ds(high, nc - high)], sem)
+
+        @pl.when(upper)
+        def _():
+            drain(ref.at[pl.ds(low, guests)], sem)
 
     for slot in range(min(2, nc)):
         drain(xs.at[slot], ex_send.at[slot])
@@ -718,12 +830,12 @@
 
         @pl.when(dist[d] > 0)
         def _():
-            drain(rr.at[d], r_send.at[d])
+            settle(rr.at[d], r_send.at[d])
             drain(rr_s.at[d], small_send.at[1 + d])
 
         @pl.when(hops[d] > 0)
         def _():
-            drain(ag.at[d], a_send.at[d])
+            settle(ag.at[d], a_send.at[d])
             drain(ag_s.at[d], small_send.at[3 + d])
 
         @pl.when(p != dest)
@@ -732,11 +844,25 @@
 
         drain(ag_s.at[d], small_send.at[7 + d])
 
-    @pl.when(p != dest)
-    def _():
-        drain(ag, o_send.at[0])
-
-    drain(ag, o_send.at[1])
+    for d in range(2):
+
+        @pl.when(p != dest)
+        def _():
+            settle_own(ag.at[d], o_send.at[0])
+
+        settle_own(ag.at[d], o_send.at[1])
+    if guests:
+
+        @pl.when(lower)
+        def _():
+            drain(gsrc, gx_send.at[0])
+
+        @pl.when(upper)
+        def _():
+            for d in range(2):
+                drain(ag.at[d, pl.ds(nc, guests)], guest_send.at[0])
+                drain(ag.at[d, pl.ds(nc, guests)], guest_send.at[1])
+
     drain(out, o_recv.at[0])
     drain(out_small, small_recv.at[0])
 
@@ -873,8 +999,10 @@
     rows_c = width // SPLIT if width % (128 * SPLIT) == 0 else width // 2
     nc, half = nblocks * (width // rows_c), rows_c // 2
     quarter = half // 2
+    guests = GUESTS if npipe == 4 else 0
+    all_c = nc + guests
     out, out_small = pl.pallas_call(
-        functools.partial(sums_kernel, npipe, ndp // 2),
+        functools.partial(sums_kernel, npipe, ndp // 2, guests),
         name="sums",
         out_shape=[ON_CHIP((nblocks, width, width), BF), ON_CHIP((64, width), BF)],
         in_specs=[anywhere, anywhere, vmem],
@@ -884,17 +1012,19 @@
             pltpu.VMEM((2, nm, nt, width), BF),
             pltpu.VMEM((rows_c, width), F32),
             pltpu.VMEM((2, half, width), BF),
-            pltpu.VMEM((nc, half, width), F32),
+            pltpu.VMEM((all_c, half, width), F32),
             pltpu.VMEM((nc, half, width), BF),
-            pltpu.VMEM((2, nc, quarter, width), BF),
-            pltpu.VMEM((2, nc, quarter, width), BF),
+            pltpu.VMEM((2, all_c, quarter, width), BF),
+            pltpu.VMEM((2, all_c, quarter, width), BF),
             pltpu.VMEM((32, width), BF),
             pltpu.VMEM((32, width), F32),
             pltpu.VMEM((32, width), BF),
             pltpu.VMEM((2, 16, width), BF),
             pltpu.VMEM((2, 16, width), BF),
-            dma((2,)), dma((2,)), dma((2,)), dma((nc + 1,)), dma((2,)), dma((2, nc + 1)), dma((2,)), dma((2, nc + 1)),
-            dma((2,)), dma((1,)), dma((9,)), dma((1,)),
+            pltpu.VMEM((max(guests, 1), half, width), BF),
+            pltpu.VMEM((max(guests, 1), half, width), BF),
+            dma((2,)), dma((2,)), dma((2,)), dma((nc + 1,)), dma((2,)), dma((2, all_c + 1)), dma((2,)), dma((2, all_c + 1)),
+            dma((2,)), dma((1,)), dma((9,)), dma((1,)), dma((1,)), dma((max(guests, 1),)), dma((2,)), pltpu.SemaphoreType.REGULAR,
         ],
         compiler_params=pltpu.CompilerParams(collective_id=1, has_side_effects=True, vmem_limit_bytes=SUMS_BYTES),
     )(xs, gs, small)

time: 366 us -> 361 us (0.986)
  Pallas kernels: 365 us -> 360 us
    pallas_call x1, Pallas kernels: 198 us -> 193 us  [body(): pl.pallas_call(functools.partial(sums_kernel, npipe, ndp // 2, guests), n...]
where the time goes in v2:
time: 361 us
  Pallas kernels  360 us (100%)
    pallas_call x1, Pallas kernels, body(): pl.pallas_call(functools.partial(sums_kernel, npipe, ndp // 2, guests), n...  193 us
    pallas_call x1, Pallas kernels, body(): pl.pallas_call(functools.partial(layers_kernel, npipe), name='layers', ou...  155 us
    pallas_call x1, Pallas kernels, body(): pl.pallas_call(widen_kernel, name='widen', out_shape=[shape((seg, width),...  11.7 us

profile of v2, /device:TPU:9, one launch (start us, length us, event | category | flops | bytes accessed | tf_op | source)
XLA Modules:
  0.0 360.6 jit_solution(16181647087794345398)
XLA Ops:
  0.7 155.2 %layers.1 = (bf16[8,1280,768]{2,1,0:T(8,128)(2,1)}, bf16[8,1280,768]{2,1,0:T(8,128)(2,1)}, f32[16,768]{1,0:T(8,128)}, f32[1,1,768]{2,1,0:T(1,128)}, f32[1,1,768]...) custom-call(bf16[1,256,768]{2,1,0:T(8,128)(2,1)} %x_hbm.1, ...), custom_call_target="tpu_custom_call" | custom-call | tf_op jit(solution)/shard_map/layers/pallas_call | solution.py:951
  155.9 0.0 copy-start
  155.9 0.0 copy-start.1
  155.9 0.0 copy-start.2
  155.9 0.0 copy-start.3
  155.9 0.0 copy-start.4
  155.9 192.7 %sums.1 = (bf16[13,768,768]{2,1,0:T(8,128)(2,1)S(1)}, bf16[64,768]{1,0:T(8,128)(2,1)S(1)}) custom-call(bf16[8,1280,768]{2,1,0:T(8,128)(2,1)} %get-tuple-element.44.x_hbm, bf16[8,1280,768]{2,1,0:T(8,128)(2,1)} %get-tuple-element.45.g_hbm, f32[16,768]{1,0:T(8,128)} %get-tuple-element.46.small), custom_call_target="tpu_custom_call" | custom-call | tf_op jit(solution)/shard_map/sums/pallas_call | solution.py:1004
  348.7 0.0 copy-done
  348.7 0.0 copy-done.1
  348.7 0.0 copy-done.2
  348.7 0.0 copy-done.3
  348.7 0.0 copy-done.4
  348.7 11.7 %widen.1 = (f32[256,768]{1,0:T(8,128)}, f32[256,768]{1,0:T(8,128)}, f32[3,768,768]{2,1,0:T(8,128)}, f32[1,768,768]{2,1,0:T(8,128)}, f32[768,3072]{1,0:T(8,128)},...) custom-call(bf16[256,768]{1,0:T(8,128)(2,1)S(1)} %copy-done, ...), custom_call_target="tpu_custom_call" | custom-call | tf_op jit(solution)/shard_map/widen/pallas_call | solution.py:1033
Async XLA Ops:
  155.9 192.8 %copy-start = (bf16[256,768]{1,0:T(8,128)(2,1)S(1)}, bf16[256,768]{1,0:T(8,128)(2,1)}, u32[]{:S(2)}) copy-start(bf16[256,768]{1,0:T(8,128)(2,1)} %get-tuple-element.42.ob) | copy-start | bytes 1179652
  155.9 192.8 %copy-start.1 = (bf16[256,768]{1,0:T(8,128)(2,1)S(1)}, bf16[256,768]{1,0:T(8,128)(2,1)}, u32[]{:S(2)}) copy-start(bf16[256,768]{1,0:T(8,128)(2,1)} %get-tuple-element.43.gb) | copy-start | bytes 1179652
  155.9 192.8 %copy-start.2 = (f32[1,2,1,768]{3,2,1,0:T(1,128)S(1)}, f32[1,2,1,768]{3,2,1,0:T(1,128)}, u32[]{:S(2)}) copy-start(f32[1,2,1,768]{3,2,1,0:T(1,128)} %get-tuple-element.51.last) | copy-start | bytes 18436
  155.9 192.8 %copy-start.3 = (f32[1,1,768]{2,1,0:T(1,128)S(1)}, f32[1,1,768]{2,1,0:T(1,128)}, u32[]{:S(2)}) copy-start(f32[1,1,768]{2,1,0:T(1,128)} %get-tuple-element.49.num) | copy-start | bytes 9220
  155.9 192.8 %copy-start.4 = (f32[1,1,768]{2,1,0:T(1,128)S(1)}, f32[1,1,768]{2,1,0:T(1,128)}, u32[]{:S(2)}) copy-start(f32[1,1,768]{2,1,0:T(1,128)} %get-tuple-element.50.den) | copy-start | bytes 9220

commit v3 on v2

--- a/solution.py
+++ b/solution.py
@@ -12,11 +12,11 @@
 BF, F32 = jnp.bfloat16, jnp.float32
 TOKENS = 128
 ROWS = 16
-SPLIT = 3
-LAG = 2
-GUESTS = 2
-GUEST_AT = 4
-GUEST_TURN = 20
+SPLIT = 6
+LAG = 3
+GUESTS = 4
+GUEST_AT = 24
+GUEST_TURN = 50
 VMEM_BYTES = 62 * 1024 * 1024
 SUMS_BYTES = 47 * 1024 * 1024
 WIDEN_BYTES = 16 * 1024 * 1024

time: 361 us -> 354 us (0.981)
  Pallas kernels: 360 us -> 352 us
    pallas_call x1, Pallas kernels: 193 us -> 186 us  [body(): pl.pallas_call(functools.partial(sums_kernel, npipe, ndp // 2, guests), n...]
where the time goes in v3:
time: 354 us; the launch traced here: 353 us
  Pallas kernels  352 us (99%)
    pallas_call x1, Pallas kernels, body(): pl.pallas_call(functools.partial(sums_kernel, npipe, ndp // 2, guests), n...  186 us
    pallas_call x1, Pallas kernels, body(): pl.pallas_call(functools.partial(layers_kernel, npipe), name='layers', ou...  155 us
    pallas_call x1, Pallas kernels, body(): pl.pallas_call(widen_kernel, name='widen', out_shape=[shape((seg, width),...  11.7 us

profile of v3, /device:TPU:9, one launch (start us, length us, event | category | flops | bytes accessed | tf_op | source)
XLA Modules:
  0.0 353.4 jit_solution(16322140030469023574)
XLA Ops:
  0.7 155.2 %layers.1 = (bf16[8,1280,768]{2,1,0:T(8,128)(2,1)}, bf16[8,1280,768]{2,1,0:T(8,128)(2,1)}, f32[16,768]{1,0:T(8,128)}, f32[1,1,768]{2,1,0:T(1,128)}, f32[1,1,768]...) custom-call(bf16[1,256,768]{2,1,0:T(8,128)(2,1)} %x_hbm.1, ...), custom_call_target="tpu_custom_call" | custom-call | tf_op jit(solution)/shard_map/layers/pallas_call | solution.py:951
  155.9 0.0 copy-start
  155.9 0.0 copy-start.1
  155.9 0.0 copy-start.2
  155.9 0.0 copy-start.3
  155.9 0.0 copy-start.4
  155.9 185.5 %sums.1 = (bf16[13,768,768]{2,1,0:T(8,128)(2,1)S(1)}, bf16[64,768]{1,0:T(8,128)(2,1)S(1)}) custom-call(bf16[8,1280,768]{2,1,0:T(8,128)(2,1)} %get-tuple-element.44.x_hbm, bf16[8,1280,768]{2,1,0:T(8,128)(2,1)} %get-tuple-element.45.g_hbm, f32[16,768]{1,0:T(8,128)} %get-tuple-element.46.small), custom_call_target="tpu_custom_call" | custom-call | tf_op jit(solution)/shard_map/sums/pallas_call | solution.py:1004
  341.5 0.0 copy-done
  341.5 0.0 copy-done.1
  341.5 0.0 copy-done.2
  341.5 0.0 copy-done.3
  341.5 0.0 copy-done.4
  341.5 11.7 %widen.1 = (f32[256,768]{1,0:T(8,128)}, f32[256,768]{1,0:T(8,128)}, f32[3,768,768]{2,1,0:T(8,128)}, f32[1,768,768]{2,1,0:T(8,128)}, f32[768,3072]{1,0:T(8,128)},...) custom-call(bf16[256,768]{1,0:T(8,128)(2,1)S(1)} %copy-done, ...), custom_call_target="tpu_custom_call" | custom-call | tf_op jit(solution)/shard_map/widen/pallas_call | solution.py:1033
Async XLA Ops:
  155.9 185.6 %copy-start = (bf16[256,768]{1,0:T(8,128)(2,1)S(1)}, bf16[256,768]{1,0:T(8,128)(2,1)}, u32[]{:S(2)}) copy-start(bf16[256,768]{1,0:T(8,128)(2,1)} %get-tuple-element.42.ob) | copy-start | bytes 1179652
  155.9 185.6 %copy-start.1 = (bf16[256,768]{1,0:T(8,128)(2,1)S(1)}, bf16[256,768]{1,0:T(8,128)(2,1)}, u32[]{:S(2)}) copy-start(bf16[256,768]{1,0:T(8,128)(2,1)} %get-tuple-element.43.gb) | copy-start | bytes 1179652
  155.9 185.6 %copy-start.2 = (f32[1,2,1,768]{3,2,1,0:T(1,128)S(1)}, f32[1,2,1,768]{3,2,1,0:T(1,128)}, u32[]{:S(2)}) copy-start(f32[1,2,1,768]{3,2,1,0:T(1,128)} %get-tuple-element.51.last) | copy-start | bytes 18436
  155.9 185.6 %copy-start.3 = (f32[1,1,768]{2,1,0:T(1,128)S(1)}, f32[1,1,768]{2,1,0:T(1,128)}, u32[]{:S(2)}) copy-start(f32[1,1,768]{2,1,0:T(1,128)} %get-tuple-element.49.num) | copy-start | bytes 9220
  155.9 185.6 %copy-start.4 = (f32[1,1,768]{2,1,0:T(1,128)S(1)}, f32[1,1,768]{2,1,0:T(1,128)}, u32[]{:S(2)}) copy-start(f32[1,1,768]{2,1,0:T(1,128)} %get-tuple-element.50.den) | copy-start | bytes 9220

commit v4 on v3

--- a/solution.py
+++ b/solution.py
@@ -14,7 +14,7 @@
 ROWS = 16
 SPLIT = 6
 LAG = 3
-GUESTS = 4
+GUESTS = 3
 GUEST_AT = 24
 GUEST_TURN = 50
 VMEM_BYTES = 62 * 1024 * 1024
@@ -104,11 +104,11 @@
     npipe,
     x_hbm, cot_hbm, gain_hbm, bias_hbm, tmix_hbm, cmix_hbm, decay_hbm, first_hbm, num_hbm, den_hbm, rows_hbm,
     win_hbm, wout_hbm, wck_hbm, wcv_hbm, wcr_hbm,
-    xo, go, small, fin_num, fin_den, fin_rows, ob, gb, turned,
+    xo, go, small, fin_num, fin_den, fin_rows, ob, gb, turned, tail,
     w, gain, bias, tmix, cmix, decay, bonus_s, num_s, den_s, rows_s, inbox, gbox,
     e_s, v_s, n_s, d_s, s_s, xh1, xh2, s2_s, c2_s, relu, r1, r2, car1, car2, back, acc, xst, gst, table, t0, t1, t2, t3,
     w_send, w_recv, in_send, in_recv, g_send, g_recv, x0_send, cot_send, ob_recv, gb_recv,
-    st_send, st_recv, fin_send, fin_recv, x_sem, go_sem, relu_sem, turn_out, turn_in,
+    st_send, st_recv, fin_send, fin_recv, x_sem, go_sem, relu_sem, turn_out, turn_in, tail_sem,
 ):
     p, i, y, k, first, s, m_chip = position()
     layer = 2 * y + m_chip
@@ -122,7 +122,7 @@
     weights = [(gain_hbm.at[0], gain), (bias_hbm.at[0], bias), (tmix_hbm, tmix), (cmix_hbm.at[0], cmix),
                (decay_hbm, decay), (first_hbm, bonus_s)]
     base = len(weights)
-    order = [0, 1, 2, 3] + [at for q in range(nq) for at in (key + q, val + q)] + [rec]
+    order = [0, 1, 2, 3] + [key + q for q in range(nq)] + [rec] + [val + q for q in range(nq)]
     source = {rec: wcr_hbm.at[0], 3: wout_hbm.at[0]}
     for c in range(3):
         source[c] = win_hbm.at[0, c]
@@ -168,8 +168,13 @@
         for a, (src, dst) in enumerate(weights[:base]):
             remote(src, dst, w_send.at[a], w_recv.at[a], 2 * y + 1 - k, i).start()
 
-    for u in range(per):
+    def give_input(u):
         give(x_hbm.at[0, pl.ds(u * nt, nt)], inbox.at[p * per + u], x0_send.at[u], in_recv.at[p * per + u], ip, ii, in_self)
+
+    @pl.when(p == 0)
+    def _():
+        give_input(0)
+
     for a, (src, dst) in enumerate(states):
         give(src, dst, st_send.at[a], st_recv.at[a], tp, ti, st_self)
 
@@ -177,14 +182,20 @@
     def _():
         for a, (src, dst) in enumerate(weights[base:]):
             remote(src, dst, w_send.at[base + a], w_recv.at[base + a], 2 * y + 1 - k, i).start()
-
-    for u in range(per):
-        give(cot_hbm.at[0, pl.ds(u * nt, nt)], gbox.at[p * per + u], cot_send.at[u], g_recv.at[p * per + u], cp, ci, cot_self)
 
     for a in range(base):
         drain(weights[a][1], w_recv.at[a])
     for a, (src, dst) in enumerate(states):
         drain(dst, st_recv.at[a])
+
+    @pl.when(p > 0)
+    def _():
+        give_input(0)
+
+    for u in range(1, per):
+        give_input(u)
+    for u in range(per):
+        give(cot_hbm.at[0, pl.ds(u * nt, nt)], gbox.at[p * per + u], cot_send.at[u], g_recv.at[p * per + u], cp, ci, cot_self)
     np_, ni = home(layer + 1, k, first)
     bp, bi = home(layer - 1, k, first)
     rate = jnp.exp(decay[...])
@@ -199,10 +210,11 @@
         for at in order:
             drain(w.at[at], w_recv.at[place[at]])
 
-        def turn(at, none):
-            slot = lax.rem(at, 2)
-
-            @pl.when(at >= 2)
+        def turn(n, none):
+            slot = lax.rem(n, 2)
+            at = lax.rem(n + val + 2, nblocks)
+
+            @pl.when(n >= 2)
             def _():
                 drain(gst.at[slot, pl.ds(0, width)], turn_out.at[slot])
 
@@ -292,9 +304,13 @@
             squares.append((r * r).astype(BF))
         ready(rec)
         t2[...] = dot(xst[slot, 5 * nt : 6 * nt], w[rec])
-        for q in range(nq):
-            ready(val + q)
-        t0[...] = dot(jnp.concatenate(squares, axis=1), w[val : val + nq].reshape(nq * width, width))
+        if begin:
+            for q in range(nq):
+                ready(val + q)
+                part = dot(squares[q], w[val + q])
+                t0[...] = part if q == 0 else t0[...] + part
+        else:
+            t0[...] = dot(jnp.concatenate(squares, axis=1), w[val : val + nq].reshape(nq * width, width))
         for r in range(0, nt, ROWS):
             here = slice(r, r + ROWS)
             gate = jax.nn.sigmoid(t2[here])
@@ -322,12 +338,13 @@
     forward(0, 0, True)
     lax.fori_loop(1, nm, forward, 0)
 
-    wanted = [at for q in range(nq) for at in (val + q, key + q)] + [rec, 3, 0, 1, 2]
+    wanted = [val + q for q in range(1, nq)] + [rec] + [key + q for q in range(nq)] + [3, 0, 1, 2]
 
     @pl.when(layer == last)
     def _():
         for at in wanted:
             local(turned.at[at], w.at[at], turn_in.at[at]).start()
+        w[val] = gst[1, 0:width]
 
     finals = ((num_s, fin_num.at[0]), (den_s, fin_den.at[0]), (rows_s, fin_rows.at[0, :, 0]))
     fp, fi = layer, first + k
@@ -389,7 +406,8 @@
                 @pl.when(layer == last)
                 def _():
                     for at in blocks:
-                        drain(w.at[at], turn_in.at[at])
+                        if at in wanted:
+                            drain(w.at[at], turn_in.at[at])
 
         if not begin:
 
@@ -465,7 +483,11 @@
         def _():
             remote(gbox.at[m], gbox.at[m], g_send.at[m], g_recv.at[m], bp, bi).start()
 
-        @pl.when(layer == 0)
+        @pl.when(jnp.logical_and(layer == 0, m == 0))
+        def _():
+            local(gbox.at[m], tail, tail_sem).start()
+
+        @pl.when(jnp.logical_and(layer == 0, m > 0))
         def _():
             q = lax.div(m, per)
             u = m - q * per
@@ -493,7 +515,7 @@
         def _():
             drain(inbox.at[m], in_send.at[m])
 
-        @pl.when(jnp.logical_not(jnp.logical_and(layer == 0, mine)))
+        @pl.when(jnp.logical_not(jnp.logical_and(layer == 0, jnp.logical_or(mine, m == 0))))
         def _():
             drain(gbox.at[m], g_send.at[m])
 
@@ -503,7 +525,8 @@
     for u in range(per):
         part = pl.ds(u * nt, nt)
         drain(ob.at[part], ob_recv.at[u])
-        drain(gb.at[part], gb_recv.at[u])
+        if u > 0:
+            drain(gb.at[part], gb_recv.at[u])
 
         @pl.when(jnp.logical_not(in_self))
         def _():
@@ -512,6 +535,14 @@
         @pl.when(jnp.logical_not(cot_self))
         def _():
             drain(cot_hbm.at[0, part], cot_send.at[u])
+
+    @pl.when(p > 0)
+    def _():
+        drain(gb.at[pl.ds(0, nt)], gb_recv.at[0])
+
+    @pl.when(layer == 0)
+    def _():
+        drain(tail, tail_sem)
 
     @pl.when(jnp.logical_not(st_self))
     def _():
@@ -533,10 +564,10 @@
 
 
 def sums_kernel(
-    npipe, ngroups, guests, x_hbm, g_hbm, small, out, out_small,
+    npipe, ngroups, guests, x_hbm, g_hbm, small, tail, out, out_small, out_tail,
     xb, gbuf, dws, xs, own, rx, rr, ag, xs_s, own_s, rx_s, rr_s, ag_s, gx, gsrc,
     x_sem, g_sem, ex_send, ex_recv, r_send, r_recv, a_send, a_recv, o_send, o_recv, small_send, small_recv,
-    gx_send, gx_recv, guest_send, guest_ready,
+    gx_send, gx_recv, guest_send, guest_ready, tail_send, tail_recv,
 ):
     p, i, y, k, first, s, m_chip = position()
     j = lax.div(i, 2)
@@ -579,8 +610,19 @@
 
         greeted = greeted + jnp.where(lower, 3, 0)
 
+    maker = jnp.logical_and(lower, m_chip == 0)
+
     def enter():
         pl.semaphore_wait(barrier, greeted)
+
+        @pl.when(jnp.logical_and(maker, k == 0))
+        def _():
+            local(tail, out_tail, tail_recv).start()
+
+        @pl.when(jnp.logical_and(maker, k > 0))
+        def _():
+            remote(tail, out_tail, tail_send, tail_recv, 0, first + 1).start()
+
         if guests:
 
             @pl.when(lower)
@@ -863,12 +905,20 @@
                 drain(ag.at[d, pl.ds(nc, guests)], guest_send.at[0])
                 drain(ag.at[d, pl.ds(nc, guests)], guest_send.at[1])
 
+    @pl.when(jnp.logical_and(maker, k > 0))
+    def _():
+        drain(tail, tail_send)
+
+    @pl.when(p == 0)
+    def _():
+        drain(out_tail, tail_recv)
+
     drain(out, o_recv.at[0])
     drain(out_small, small_recv.at[0])
 
 
 def widen_kernel(
-    ob, gb, rows, w, num, den, last,
+    ob, gb, rows, w, tail, num, den, last,
     out, grad, g_in, g_out, g_key, g_val, g_rec, gain, bias, tmix, cmix, decay, bonus, fin_num, fin_den, fin_rows,
     stage, narrow, wide, sem, in_sem, out_sem,
 ):
@@ -917,6 +967,12 @@
     for n, dst in enumerate((out, grad)):
         drain(narrow.at[n], in_sem.at[n])
         wide[n] = narrow[n].astype(F32)
+        if n == 1:
+
+            @pl.when(lax.axis_index("pipe") == 0)
+            def _():
+                wide[n, 0 : tail.shape[0]] = tail[...].astype(F32)
+
         local(wide.at[n], dst, out_sem.at[n]).start()
     at = 0
     for dst in (gain, bias, tmix, cmix, decay, bonus):
@@ -948,7 +1004,7 @@
     shape = jax.ShapeDtypeStruct
     nb = 6 + nq
     nblocks = 5 + 2 * nq
-    xs, gs, small, fin_num, fin_den, fin_rows, ob, gb, turned = pl.pallas_call(
+    xs, gs, small, fin_num, fin_den, fin_rows, ob, gb, turned, tail = pl.pallas_call(
         functools.partial(layers_kernel, npipe),
         name="layers",
         out_shape=[
@@ -961,9 +1017,10 @@
             shape((seg, width), BF),
             shape((seg, width), BF),
             shape((nblocks, width, width), BF),
+            shape((nt, width), BF),
         ],
         in_specs=[anywhere] * 16,
-        out_specs=[anywhere, anywhere, vmem] + [anywhere] * 6,
+        out_specs=[anywhere, anywhere, vmem] + [anywhere] * 7,
         scratch_shapes=[
             pltpu.VMEM((nblocks, width, width), BF),
             pltpu.VMEM((2, width), F32),
@@ -990,7 +1047,7 @@
             *[pltpu.VMEM((nt, width), F32)] * 4,
             dma((6 + nblocks,)), dma((6 + nblocks,)), dma((nm,)), dma((nm,)), dma((nm,)), dma((nm,)),
             dma((per,)), dma((per,)), dma((per,)), dma((per,)),
-            dma((3,)), dma((3,)), dma((3,)), dma((3,)), dma((2,)), dma((2,)), dma((nm,)), dma((2,)), dma((nblocks,)),
+            dma((3,)), dma((3,)), dma((3,)), dma((3,)), dma((2,)), dma((2,)), dma((nm,)), dma((2,)), dma((nblocks,)), dma,
         ],
         compiler_params=pltpu.CompilerParams(collective_id=0, has_side_effects=True, vmem_limit_bytes=VMEM_BYTES),
     )(block_input, cotangent, ln_gain, ln_bias, jnp.swapaxes(tm_mix, 0, 1), cm_mix, time_decay, time_first, wkv_num, wkv_den, last_rows,
@@ -1001,12 +1058,12 @@
     quarter = half // 2
     guests = GUESTS if npipe == 4 else 0
     all_c = nc + guests
-    out, out_small = pl.pallas_call(
+    out, out_small, out_tail = pl.pallas_call(
         functools.partial(sums_kernel, npipe, ndp // 2, guests),
         name="sums",
-        out_shape=[ON_CHIP((nblocks, width, width), BF), ON_CHIP((64, width), BF)],
-        in_specs=[anywhere, anywhere, vmem],
-        out_specs=[vmem, vmem],
+        out_shape=[ON_CHIP((nblocks, width, width), BF), ON_CHIP((64, width), BF), ON_CHIP((nt, width), BF)],
+        in_specs=[anywhere, anywhere, vmem, anywhere],
+        out_specs=[vmem, vmem, vmem],
         scratch_shapes=[
             pltpu.VMEM((2, nm, nt, rows_c), BF),
             pltpu.VMEM((2, nm, nt, width), BF),
@@ -1024,10 +1081,10 @@
             pltpu.VMEM((max(guests, 1), half, width), BF),
             pltpu.VMEM((max(guests, 1), half, width), BF),
             dma((2,)), dma((2,)), dma((2,)), dma((nc + 1,)), dma((2,)), dma((2, all_c + 1)), dma((2,)), dma((2, all_c + 1)),
-            dma((2,)), dma((1,)), dma((9,)), dma((1,)), dma((1,)), dma((max(guests, 1),)), dma((2,)), pltpu.SemaphoreType.REGULAR,
+            dma((2,)), dma((1,)), dma((9,)), dma((1,)), dma((1,)), dma((max(guests, 1),)), dma((2,)), pltpu.SemaphoreType.REGULAR, dma, dma,
         ],
         compiler_params=pltpu.CompilerParams(collective_id=1, has_side_effects=True, vmem_limit_bytes=SUMS_BYTES),
-    )(xs, gs, small)
+    )(xs, gs, small, tail)
 
     in_vmem = pltpu.with_memory_space_constraint(out, pltpu.VMEM)
     wide = pl.pallas_call(
@@ -1040,7 +1097,7 @@
             shape((1, width), F32), shape((1, width), F32),
             shape((1, 1, width), F32), shape((1, 1, width), F32), shape((1, 2, 1, width), F32),
         ],
-        in_specs=[anywhere, anywhere, vmem, vmem, vmem, vmem, vmem],
+        in_specs=[anywhere, anywhere, vmem, vmem, vmem, vmem, vmem, vmem],
         out_specs=[anywhere] * 7 + [vmem] * 9,
         scratch_shapes=[
             pltpu.VMEM((4, width // 2, width), F32),
@@ -1049,7 +1106,7 @@
             dma((4,)), dma((2,)), dma((2,)),
         ],
         compiler_params=pltpu.CompilerParams(vmem_limit_bytes=WIDEN_BYTES),
-    )(ob, gb, out_small, in_vmem, fin_num, fin_den, fin_rows)
+    )(ob, gb, out_small, in_vmem, out_tail, fin_num, fin_den, fin_rows)
     return (
         wide[0][None],
         wide[1][None],

time: 354 us -> 351 us (level)
  no operation moved by 1% of the time
where the time goes in v4:
time: 351 us; the launch traced here: 350 us
  Pallas kernels  349 us (99%)
    pallas_call x1, Pallas kernels, body(): pl.pallas_call(functools.partial(sums_kernel, npipe, ndp // 2, guests), n...  185 us
    pallas_call x1, Pallas kernels, body(): pl.pallas_call(functools.partial(layers_kernel, npipe), name='layers', ou...  152 us
    pallas_call x1, Pallas kernels, body(): pl.pallas_call(widen_kernel, name='widen', out_shape=[shape((seg, width),...  11.7 us

profile of v4, /device:TPU:9, one launch (start us, length us, event | category | flops | bytes accessed | tf_op | source)
XLA Modules:
  0.0 349.7 jit_solution(13993053497379956047)
XLA Ops:
  0.7 152.4 %layers.1 = (bf16[8,1280,768]{2,1,0:T(8,128)(2,1)}, bf16[8,1280,768]{2,1,0:T(8,128)(2,1)}, f32[16,768]{1,0:T(8,128)}, f32[1,1,768]{2,1,0:T(1,128)}, f32[1,1,768]...) custom-call(bf16[1,256,768]{2,1,0:T(8,128)(2,1)} %x_hbm.1, ...), custom_call_target="tpu_custom_call" | custom-call | tf_op jit(solution)/shard_map/layers/pallas_call | solution.py:1007
  153.1 0.0 copy-start
  153.1 0.0 copy-start.1
  153.1 0.0 copy-start.2
  153.1 0.0 copy-start.3
  153.1 0.0 copy-start.4
  153.1 184.7 %sums.1 = (bf16[13,768,768]{2,1,0:T(8,128)(2,1)S(1)}, bf16[64,768]{1,0:T(8,128)(2,1)S(1)}, bf16[128,768]{1,0:T(8,128)(2,1)S(1)}) custom-call(bf16[8,1280,768]{2,1,0:T(8,128)(2,1)} %get-tuple-element.46.x_hbm, bf16[8,1280,768]{2,1,0:T(8,128)(2,1)} %get-tuple-element.47.g_hbm, f32[16,768]{1,0:T(8,128)} %get-tuple-element.48.small, ...), custom_call_target="tpu_custom_call" | custom-call | tf_op jit(solution)/shard_map/sums/pallas_call | solution.py:1061
  337.8 0.0 copy-done
  337.8 0.0 copy-done.1
  337.8 0.0 copy-done.2
  337.8 0.0 copy-done.3
  337.8 0.0 copy-done.4
  337.8 11.7 %widen.1 = (f32[256,768]{1,0:T(8,128)}, f32[256,768]{1,0:T(8,128)}, f32[3,768,768]{2,1,0:T(8,128)}, f32[1,768,768]{2,1,0:T(8,128)}, f32[768,3072]{1,0:T(8,128)},...) custom-call(bf16[256,768]{1,0:T(8,128)(2,1)S(1)} %copy-done, ...), custom_call_target="tpu_custom_call" | custom-call | tf_op jit(solution)/shard_map/widen/pallas_call | solution.py:1090
Async XLA Ops:
  153.1 184.7 %copy-start = (bf16[256,768]{1,0:T(8,128)(2,1)S(1)}, bf16[256,768]{1,0:T(8,128)(2,1)}, u32[]{:S(2)}) copy-start(bf16[256,768]{1,0:T(8,128)(2,1)} %get-tuple-element.44.ob) | copy-start | bytes 1179652
  153.1 184.7 %copy-start.1 = (bf16[256,768]{1,0:T(8,128)(2,1)S(1)}, bf16[256,768]{1,0:T(8,128)(2,1)}, u32[]{:S(2)}) copy-start(bf16[256,768]{1,0:T(8,128)(2,1)} %get-tuple-element.45.gb) | copy-start | bytes 1179652
  153.1 184.7 %copy-start.2 = (f32[1,2,1,768]{3,2,1,0:T(1,128)S(1)}, f32[1,2,1,768]{3,2,1,0:T(1,128)}, u32[]{:S(2)}) copy-start(f32[1,2,1,768]{3,2,1,0:T(1,128)} %get-tuple-element.55.last) | copy-start | bytes 18436
  153.1 184.7 %copy-start.3 = (f32[1,1,768]{2,1,0:T(1,128)S(1)}, f32[1,1,768]{2,1,0:T(1,128)}, u32[]{:S(2)}) copy-start(f32[1,1,768]{2,1,0:T(1,128)} %get-tuple-element.53.num) | copy-start | bytes 9220
  153.1 184.7 %copy-start.4 = (f32[1,1,768]{2,1,0:T(1,128)S(1)}, f32[1,1,768]{2,1,0:T(1,128)}, u32[]{:S(2)}) copy-start(f32[1,1,768]{2,1,0:T(1,128)} %get-tuple-element.54.den) | copy-start | bytes 9220

commit v5 on v4

--- a/solution.py
+++ b/solution.py
@@ -133,11 +133,6 @@
     place = {at: base + n for n, at in enumerate(order)}
     owner = k == m_chip
 
-    @pl.when(owner)
-    def _():
-        for a, (src, dst) in enumerate(weights):
-            local(src, dst, w_recv.at[a]).start()
-
     barrier = pltpu.get_barrier_semaphore()
     for step in range(1, 2 * npipe):
         at = lax.rem(2 * p + s + step, 2 * npipe)
@@ -168,6 +163,16 @@
         for a, (src, dst) in enumerate(weights[:base]):
             remote(src, dst, w_send.at[a], w_recv.at[a], 2 * y + 1 - k, i).start()
 
+    @pl.when(owner)
+    def _():
+        for a, (src, dst) in enumerate(weights[base:]):
+            remote(src, dst, w_send.at[base + a], w_recv.at[base + a], 2 * y + 1 - k, i).start()
+
+    @pl.when(owner)
+    def _():
+        for a, (src, dst) in enumerate(weights):
+            local(src, dst, w_recv.at[a]).start()
+
     def give_input(u):
         give(x_hbm.at[0, pl.ds(u * nt, nt)], inbox.at[p * per + u], x0_send.at[u], in_recv.at[p * per + u], ip, ii, in_self)
 
@@ -177,11 +182,6 @@
 
     for a, (src, dst) in enumerate(states):
         give(src, dst, st_send.at[a], st_recv.at[a], tp, ti, st_self)
-
-    @pl.when(owner)
-    def _():
-        for a, (src, dst) in enumerate(weights[base:]):
-            remote(src, dst, w_send.at[base + a], w_recv.at[base + a], 2 * y + 1 - k, i).start()
 
     for a in range(base):
         drain(weights[a][1], w_recv.at[a])

time: 351 us -> 350 us (level)
  no operation moved by 1% of the time
where the time goes in v5:
time: 350 us; the launch traced here: 349 us
  Pallas kernels  348 us (99%)
    pallas_call x1, Pallas kernels, body(): pl.pallas_call(functools.partial(sums_kernel, npipe, ndp // 2, guests), n...  185 us
    pallas_call x1, Pallas kernels, body(): pl.pallas_call(functools.partial(layers_kernel, npipe), name='layers', ou...  152 us
    pallas_call x1, Pallas kernels, body(): pl.pallas_call(widen_kernel, name='widen', out_shape=[shape((seg, width),...  11.7 us

profile of v5, /device:TPU:9, one launch (start us, length us, event | category | flops | bytes accessed | tf_op | source)
XLA Modules:
  0.0 349.1 jit_solution(9629231126605135754)
XLA Ops:
  0.7 151.7 %layers.1 = (bf16[8,1280,768]{2,1,0:T(8,128)(2,1)}, bf16[8,1280,768]{2,1,0:T(8,128)(2,1)}, f32[16,768]{1,0:T(8,128)}, f32[1,1,768]{2,1,0:T(1,128)}, f32[1,1,768]...) custom-call(bf16[1,256,768]{2,1,0:T(8,128)(2,1)} %x_hbm.1, ...), custom_call_target="tpu_custom_call" | custom-call | tf_op jit(solution)/shard_map/layers/pallas_call | solution.py:1007
  152.4 0.0 copy-start
  152.4 0.0 copy-start.1
  152.4 0.0 copy-start.2
  152.4 0.0 copy-start.3
  152.4 0.0 copy-start.4
  152.4 184.7 %sums.1 = (bf16[13,768,768]{2,1,0:T(8,128)(2,1)S(1)}, bf16[64,768]{1,0:T(8,128)(2,1)S(1)}, bf16[128,768]{1,0:T(8,128)(2,1)S(1)}) custom-call(bf16[8,1280,768]{2,1,0:T(8,128)(2,1)} %get-tuple-element.46.x_hbm, bf16[8,1280,768]{2,1,0:T(8,128)(2,1)} %get-tuple-element.47.g_hbm, f32[16,768]{1,0:T(8,128)} %get-tuple-element.48.small, ...), custom_call_target="tpu_custom_call" | custom-call | tf_op jit(solution)/shard_map/sums/pallas_call | solution.py:1061
  337.1 0.0 copy-done
  337.1 0.0 copy-done.1
  337.2 0.0 copy-done.2
  337.2 0.0 copy-done.3
  337.2 0.0 copy-done.4
  337.2 11.7 %widen.1 = (f32[256,768]{1,0:T(8,128)}, f32[256,768]{1,0:T(8,128)}, f32[3,768,768]{2,1,0:T(8,128)}, f32[1,768,768]{2,1,0:T(8,128)}, f32[768,3072]{1,0:T(8,128)},...) custom-call(bf16[256,768]{1,0:T(8,128)(2,1)S(1)} %copy-done, ...), custom_call_target="tpu_custom_call" | custom-call | tf_op jit(solution)/shard_map/widen/pallas_call | solution.py:1090
Async XLA Ops:
  152.4 184.7 %copy-start = (bf16[256,768]{1,0:T(8,128)(2,1)S(1)}, bf16[256,768]{1,0:T(8,128)(2,1)}, u32[]{:S(2)}) copy-start(bf16[256,768]{1,0:T(8,128)(2,1)} %get-tuple-element.44.ob) | copy-start | bytes 1179652
  152.4 184.7 %copy-start.1 = (bf16[256,768]{1,0:T(8,128)(2,1)S(1)}, bf16[256,768]{1,0:T(8,128)(2,1)}, u32[]{:S(2)}) copy-start(bf16[256,768]{1,0:T(8,128)(2,1)} %get-tuple-element.45.gb) | copy-start | bytes 1179652
  152.4 184.7 %copy-start.2 = (f32[1,2,1,768]{3,2,1,0:T(1,128)S(1)}, f32[1,2,1,768]{3,2,1,0:T(1,128)}, u32[]{:S(2)}) copy-start(f32[1,2,1,768]{3,2,1,0:T(1,128)} %get-tuple-element.55.last) | copy-start | bytes 18436
  152.4 184.7 %copy-start.3 = (f32[1,1,768]{2,1,0:T(1,128)S(1)}, f32[1,1,768]{2,1,0:T(1,128)}, u32[]{:S(2)}) copy-start(f32[1,1,768]{2,1,0:T(1,128)} %get-tuple-element.53.num) | copy-start | bytes 9220
  152.4 184.7 %copy-start.4 = (f32[1,1,768]{2,1,0:T(1,128)S(1)}, f32[1,1,768]{2,1,0:T(1,128)}, u32[]{:S(2)}) copy-start(f32[1,1,768]{2,1,0:T(1,128)} %get-tuple-element.54.den) | copy-start | bytes 9220
